TPU v7x, 128 devices: a whole 4x4x4 slice. The times are simulated.
128 devices in a mesh: band: 64 (over z, y, x), feat: 2 (over core).
Axes of the slice: x: 4, y: 4, z: 4, core: 2. Of those that a mesh axis runs over, the one named last changes fastest.
Arguments:
- grid_latent: bfloat16 [65536, 512], P('band'), may hold values from -6 to 6
- mesh_latent: bfloat16 [16384, 512], P('band', 'feat'), may hold values from -6 to 6
- grid_in_w: bfloat16 [512, 512], P(None, 'feat'), may hold values from -0.25 to 0.25
- grid_bias: bfloat16 [512], P('feat'), may hold values from -3 to 3
- g2m_src: int32 [64, 64, 64], P('band'), may hold values from 0 to 1023
- g2m_dst: int32 [64, 64, 64], P('band'), may hold values from 0 to 255
- g2m_weight: bfloat16 [64, 64, 64], P('band'), may hold values from 0 to 2, as said below
- mesh_src: int32 [64, 12288], P('band'), may hold values from 0 to 383
- mesh_dst: int32 [64, 12288], P('band'), may hold values from 0 to 255
- halo_index: int32 [64, 2, 64], P('band'), may hold values from 0 to 255
- edge_send_w: bfloat16 [2, 512, 512], P(None, None, 'feat'), may hold values from -0.25 to 0.25
- edge_recv_w: bfloat16 [2, 512, 512], P(None, None, 'feat'), may hold values from -0.25 to 0.25
- edge_bias: bfloat16 [2, 512], P(None, 'feat'), may hold values from -3 to 3
- node_in_w: bfloat16 [3, 1024, 512], P(None, None, 'feat'), may hold values from -0.125 to 0.125
- node_bias: bfloat16 [3, 512], P(None, 'feat'), may hold values from -3 to 3
- node_out_w: bfloat16 [3, 512, 512], P(None, 'feat'), may hold values from -0.25 to 0.25
Outputs:
- mesh_out: bfloat16 [16384, 512], P('band', 'feat')
Inputs may be any that keep to these rules, and one draw needn't show every extreme that they name: `g2m_weight`: each pair of band s and partition d has a live count of 48 to 64: slots c below it have positive weights, the others weight 0. A partition's slots from its own band are all live.
All inputs are finite; a program needn't handle non-finite values.
Results may differ from a plain program's by a relative error of at most 0.029.
Values may be sent and summed in bfloat16 or wider, within the bound.
No kernel may reach another device: no remote copies, remote signals or barrier semaphores. Data moves between devices by JAX's collectives and lax.ppermute only.
A program may use at most 64 MiB of HBM per device.

v0:
```python
import functools

import jax
import jax.numpy as jnp
from jax import lax
from jax.experimental import pallas as pl
from jax.experimental.pallas import tpu as pltpu
from jax.sharding import PartitionSpec as P

VMEM = pl.BlockSpec(memory_space=pltpu.VMEM)
SMEM = pl.BlockSpec(memory_space=pltpu.SMEM)
F32 = jnp.float32
BF16 = jnp.bfloat16


def dot32(a, b):
    return jnp.dot(a, b, preferred_element_type=F32)


def dot32_nt(a, b):
    return lax.dot_general(a, b, (((1,), (1,)), ((), ())), preferred_element_type=F32)


def silu(v):
    half = 0.5 * v
    return half + half * jnp.tanh(half)


LANES = 128
BLOCK = 768


def head_of(edges):
    return edges * 7 // 16 // BLOCK * BLOCK


def over_blocks(edges, work):
    def step(i, carry):
        work(pl.ds(pl.multiple_of(i * BLOCK, BLOCK), BLOCK))
        return carry

    lax.fori_loop(0, edges // BLOCK, step, 0)


def one_hot_columns(row, count):
    ids = lax.broadcasted_iota(jnp.int32, (count, row.shape[1]), 0).astype(jnp.int16)
    return jnp.where(ids == row.astype(jnp.int16), jnp.ones((), BF16), jnp.zeros((), BF16))


def call(kernel, name, out_shape, in_specs, flops, limit=24, scratch=()):
    many = isinstance(out_shape, tuple)
    return pl.pallas_call(
        kernel,
        name=name,
        out_shape=out_shape,
        in_specs=in_specs,
        out_specs=(VMEM,) * len(out_shape) if many else VMEM,
        scratch_shapes=scratch,
        compiler_params=pltpu.CompilerParams(vmem_limit_bytes=limit * 2**20),
        cost_estimate=pl.CostEstimate(flops=flops, bytes_accessed=2**20, transcendentals=0),
    )


def embed_kernel(grid, weights, bias, source, rows_out):
    bands, slots, _ = rows_out.shape
    count = grid.shape[0]
    add = bias[...].astype(F32).reshape(1, bias.shape[0])
    embedding = silu(dot32(grid[...], weights[...]) + add).astype(BF16)
    columns = source[0].T
    ids = lax.broadcasted_iota(jnp.int32, (slots, count), 1)
    group = 8 if bands % 8 == 0 else 1
    for first in range(0, bands, group):
        chosen = [
            jnp.where(ids == columns[:, band : band + 1], jnp.ones((), BF16), jnp.zeros((), BF16))
            for band in range(first, first + group)
        ]
        part = dot32(jnp.concatenate(chosen, 0), embedding).astype(BF16)
        rows_out[first : first + group] = part.reshape(group, slots, part.shape[1])


def slots_kernel(node, weight, rows, aggregate):
    ids = lax.broadcasted_iota(jnp.int32, (aggregate.shape[0], node.shape[1]), 0)
    chosen = ids.astype(jnp.int16) == node[...].astype(jnp.int16)
    matrix = jnp.where(chosen, weight[...], jnp.zeros((), BF16))
    aggregate[...] = dot32(matrix, rows[...]).astype(BF16)


def own_terms_kernel(core, state, mine, in_mine, in_other, bias_mine, bias_other, sum_mine, sum_other):
    wide, narrow = state.shape[1], mine.shape[1]
    rows = pl.ds(pl.multiple_of(wide + core[0] * narrow, narrow), narrow)
    for weights, bias, total in ((in_mine, bias_mine, sum_mine), (in_other, bias_other, sum_other)):
        own = dot32(mine[...], weights[rows, :])
        total[...] = dot32(state[...], weights[:wide, :]) + own + bias[...]


def hidden_units(core, other, in_mine, in_other, sum_mine, sum_other):
    narrow = other.shape[1]
    wide = in_mine.shape[0] - 2 * narrow
    rows = pl.ds(pl.multiple_of(wide + (1 - core[0]) * narrow, narrow), narrow)
    hidden_mine = silu(sum_mine[...] + dot32(other[...], in_mine[rows, :]))
    hidden_other = silu(sum_other[...] + dot32(other[...], in_other[rows, :]))
    return hidden_mine.astype(BF16), hidden_other.astype(BF16)


def node_kernel(
    core, state, other, in_mine, in_other, sum_mine, sum_other, out_mine, out_other,
    send_w, edge_bias, halo_hot, state_out, sender_out, one_out, two_out,
):
    hidden_mine, hidden_other = hidden_units(core, other, in_mine, in_other, sum_mine, sum_other)
    update = dot32(hidden_mine, out_mine[...]) + dot32(hidden_other, out_other[...])
    after = (state[...].astype(F32) + update).astype(BF16)
    state_out[...] = after
    sender = (dot32(after, send_w[...]) + edge_bias[...]).astype(BF16)
    sender_out[...] = sender
    leaving = dot32(halo_hot[...], sender).astype(BF16)
    width = one_out.shape[0]
    one_out[...] = leaving[:width]
    two_out[...] = leaving[width:]


def last_kernel(
    core, state, other, in_mine, in_other, sum_mine, sum_other, out_mine, out_other, result
):
    hidden_mine, hidden_other = hidden_units(core, other, in_mine, in_other, sum_mine, sum_other)
    update = dot32(hidden_mine, out_mine[...]) + dot32(hidden_other, out_other[...])
    narrow = result.shape[1]
    before = jnp.where(core[0] == 0, state[:, :narrow], state[:, narrow:])
    result[...] = (before.astype(F32) + update).astype(BF16)


def local_kernel(few, keys, sender, state, recv_w, pre, partial):
    nodes = sender.shape[0]
    shift = nodes.bit_length() - 1
    head = head_of(keys.shape[1])
    receiver = dot32(state[...], recv_w[...]).astype(BF16)
    table = jnp.concatenate([sender[...].T, receiver.T], 1)

    def gather(edges):
        to = one_hot_columns(keys[:, edges] & (nodes - 1), nodes)
        chosen = jnp.concatenate([one_hot_columns(keys[:, edges] >> shift, nodes), to], 0)
        return dot32(table, chosen), to

    @pl.when(few[0] == 1)
    def _():
        sums, to = gather(slice(0, head))
        messages = silu(sums).astype(BF16)
        pre[:, head:] = gather(slice(head, None))[0]
        partial[...] = dot32_nt(to, messages)

    @pl.when(few[0] != 1)
    def _():
        def block(edges):
            pre[:, edges] = gather(edges)[0]

        over_blocks(keys.shape[1], block)


def halo_kernel(few, keys, pre, partial, one, two, aggregate, total):
    nodes = aggregate.shape[0]
    shift = nodes.bit_length() - 1
    head = head_of(keys.shape[1])
    table = jnp.concatenate([one[...], two[...]], 0).T

    def sums_of(edges):
        source = (keys[:, edges] >> shift) - nodes
        sums = pre[:, edges] + dot32(table, one_hot_columns(source, table.shape[1]))
        to = one_hot_columns(keys[:, edges] & (nodes - 1), nodes)
        return dot32_nt(to, silu(sums).astype(BF16))

    @pl.when(few[0] == 1)
    def _():
        total[...] = partial[...]

    @pl.when(few[0] != 1)
    def _():
        def block(edges):
            total[...] += sums_of(edges)

        total[...] = jnp.zeros_like(total)
        over_blocks(head, block)

    aggregate[...] = (total[...] + sums_of(slice(head, None))).astype(BF16)


def swap_cores(value):
    return lax.ppermute(value, "feat", [(0, 1), (1, 0)])


def body(
    grid_latent,
    mesh_latent,
    grid_in_w,
    grid_bias,
    g2m_src,
    g2m_dst,
    g2m_weight,
    mesh_src,
    mesh_dst,
    halo_index,
    edge_send_w,
    edge_recv_w,
    edge_bias,
    node_in_w,
    node_bias,
    node_out_w,
):
    feature_width = grid_in_w.shape[1]
    nodes = mesh_latent.shape[0]
    edges = mesh_src.shape[1]
    halo = halo_index.shape[2]
    partitions = lax.axis_size("band")
    core = lax.axis_index("feat").astype(jnp.int32).reshape(1)
    part = lax.axis_index("band")
    band_count = g2m_src.shape[1]
    slot_count = g2m_src.shape[2]
    slots = band_count * slot_count
    outgoing = call(
        embed_kernel,
        "embed",
        jax.ShapeDtypeStruct((band_count, slot_count, feature_width), BF16),
        [VMEM] * 4,
        2 * slots * grid_latent.shape[0] * feature_width,
        limit=60,
    )(grid_latent, grid_in_w, grid_bias, g2m_src)
    incoming = lax.all_to_all(outgoing, "band", split_axis=0, concat_axis=0, tiled=True)

    _, latent, in_mine, bias_mine, out_mine = lax.optimization_barrier(
        (outgoing, mesh_latent, node_in_w, node_bias, node_out_w)
    )
    layers, deep, _ = node_in_w.shape
    wide = node_out_w.shape[2]
    state = lax.all_gather(latent, "feat", axis=1, tiled=True)
    in_other, bias_other, out_other = swap_cores(in_mine), swap_cores(bias_mine), swap_cores(out_mine)
    node_w = []
    for layer in range(layers):
        out_w = [out_mine[layer], out_other[layer]]
        if layer + 1 == layers:
            first = core[0] * feature_width
            out_w = [lax.dynamic_slice_in_dim(w, first, feature_width, 1) for w in out_w]
        biases = [b[layer].astype(F32)[None] for b in (bias_mine, bias_other)]
        node_w.append((in_mine[layer], in_other[layer], *biases, *out_w))
    edge_w = [
        (edge_send_w[step], edge_recv_w[step], edge_bias[step].astype(F32)[None])
        for step in range(layers - 1)
    ]
    odd = part % 2 == 1
    to_next, to_previous = halo_index[0, 0], halo_index[0, 1]
    leaving = jnp.concatenate(
        [jnp.where(odd, to_next, to_previous), jnp.where(odd, to_previous, to_next)]
    )
    halo_ids = lax.broadcasted_iota(jnp.int32, (2 * halo, nodes), 1)
    halo_hot = (leaving[:, None] == halo_ids).astype(BF16)
    from_previous = (mesh_src >= nodes) & (mesh_src < nodes + halo)
    from_next = mesh_src >= nodes + halo
    source = mesh_src + jnp.where(
        odd & from_previous, halo, jnp.where(odd & from_next, -halo, 0)
    )
    outside = (from_previous & (part == 0)) | (from_next & (part == partitions - 1))
    source = jnp.where(outside, nodes + 2 * halo, source)
    keys = (source * nodes + mesh_dst).reshape(edges // LANES, LANES)
    keys = lax.sort(keys, dimension=0)
    last = keys[head_of(edges) // LANES - 1]
    few_halo = (jnp.max(last) < nodes * nodes).astype(jnp.int32).reshape(1)
    keys = keys.reshape(1, edges)
    slot_node, slot_weight = g2m_dst.reshape(1, slots), g2m_weight.reshape(1, slots)
    incoming, core, state, node_w, edge_w, halo_hot, keys, few_halo, slot_node, slot_weight = (
        lax.optimization_barrier(
            (incoming, core, state, node_w, edge_w, halo_hot, keys, few_halo, slot_node, slot_weight)
        )
    )
    half = jax.ShapeDtypeStruct((nodes, feature_width), BF16)
    aggregate = call(
        slots_kernel,
        "slots",
        half,
        [VMEM] * 3,
        2 * slots * nodes * feature_width,
    )(slot_node, slot_weight, incoming.reshape(slots, -1))

    cores = lax.axis_size("feat")
    pairs_two = [(i, i ^ 1) for i in range(partitions)]
    pairs_one = []
    for i in range(partitions):
        other = ((i - 1) ^ 1) + 1
        for c in range(cores):
            end = i == 0 or other >= partitions
            partner = i * cores + (c ^ 1) if end else other * cores + c
            pairs_one.append((i * cores + c, partner))
    halo_rows = jax.ShapeDtypeStruct((halo, feature_width), BF16)
    node_flops = 2 * nodes * wide * (deep + wide)
    for layer in range(layers):
        in_one, in_two, bias_one, bias_two, out_one, out_two = node_w[layer]
        total = jax.ShapeDtypeStruct((nodes, feature_width), F32)
        other = swap_cores(aggregate)
        totals = call(
            own_terms_kernel, "own_terms", (total, total), [SMEM] + [VMEM] * 6, node_flops // 2
        )(core, state, aggregate, in_one, in_two, bias_one, bias_two)
        operands = (core, state, other, in_one, in_two, *totals, out_one, out_two)
        if layer + 1 == layers:
            return call(last_kernel, "node_last", half, [SMEM] + [VMEM] * 8, node_flops)(*operands)
        send_w, recv_w, sender_bias = edge_w[layer]
        state, sender, leaving_one, leaving_two = call(
            node_kernel,
            "node",
            (jax.ShapeDtypeStruct((nodes, wide), BF16), half, halo_rows, halo_rows),
            [SMEM] + [VMEM] * 11,
            node_flops,
        )(*operands, send_w, sender_bias, halo_hot)
        arrived_one = lax.ppermute(leaving_one, ("band", "feat"), pairs_one)
        arrived_two = lax.ppermute(leaving_two, "band", pairs_two)
        pre, partial = call(
            local_kernel,
            "edge_local",
            (pltpu.VMEM((feature_width, edges), F32), total),
            [SMEM] + [VMEM] * 4,
            4 * edges * nodes * feature_width,
        )(few_halo, keys, sender, state, recv_w)
        aggregate = call(
            halo_kernel,
            "edge_halo",
            half,
            [SMEM] + [VMEM] * 5,
            3 * edges * nodes * feature_width,
            scratch=[pltpu.VMEM((nodes, feature_width), F32)],
        )(few_halo, keys, pre, partial, arrived_one, arrived_two)


def solution(mesh):
    in_specs = (
        P("band", None),
        P("band", "feat"),
        P(None, "feat"),
        P("feat"),
        P("band", None, None),
        P("band", None, None),
        P("band", None, None),
        P("band", None),
        P("band", None),
        P("band", None, None),
        P(None, None, "feat"),
        P(None, None, "feat"),
        P(None, "feat"),
        P(None, None, "feat"),
        P(None, "feat"),
        P(None, "feat", None),
    )
    out_specs = P("band", "feat")
    return jax.shard_map(body, mesh=mesh, in_specs=in_specs, out_specs=out_specs, check_vma=False)
```

profile of v0, /device:TPU:1, one launch (start us, length us, event | category | flops | bytes accessed | tf_op | source)
XLA Modules:
  0.0 75.2 jit_solution(6284916250766798543)
XLA Ops:
  0.0 5.4 %embed.1 = bf16[64,64,256]{2,1,0:T(8,128)(2,1)} custom-call(bf16[1024,512]{1,0:T(8,128)(2,1)} %grid.1, bf16[512,256]{1,0:T(8,128)(2,1)} %weights.1, bf16[256]{0:T(256)(128)(2,1)} %bias.1, s32[1,64,64]{2,1,0:T(8,128)} %source.1), custom_call_target="tpu_custom_call" | custom-call | flops 2147483648 | bytes 1048576 | tf_op jit(solution)/shard_map/embed/pallas_call | solution.py:217
  5.4 12.1 %all-to-all-start = ((bf16[64,64,256]{2,1,0:T(8,128)(2,1)}), bf16[64,64,256]{2,1,0:T(8,128)(2,1)S(1)}, u32[]{:S(2)}, u32[]{:S(2)}) async-start(bf16[64,64,256]{2,1,0:T(8,128)(2,1)} %embed.1), calls=%async_computation | async-start | bytes 4194304 | tf_op jit(solution)/shard_map/all_to_all | solution.py:225
  17.5 0.0 copy-start.23
  17.5 0.0 copy-start.24
  17.5 1.0 %collective-permute-start.1 = (bf16[3,256]{1,0:T(4,128)(2,1)}, bf16[3,256]{1,0:T(4,128)(2,1)}, u32[]{:S(2)}, u32[]{:S(2)}) collective-permute-start(bf16[3,256]{1,0:T(4,128)(2,1)} %param.30), channel_id=1, source_target_pairs={{0,1},{1,0},{2,3},{3,2},{4,5},{5,4},{6,7},{7,6},{8,9},{9,8},{10,11... | collective-permute-start | bytes 4616 | tf_op jit(solution)/shard_map/ppermute | solution.py:186
  18.5 0.1 collective-permute-start.2
  18.6 0.4 collective-permute-start
  19.0 2.0 %fusion.5 = (bf16[1,256,512]{2,1,0:T(8,128)(2,1)S(1)}, bf16[256,512]{1,0:T(8,128)(2,1)}, bf16[256,512]{1,0:T(8,128)(2,1)}) fusion(bf16[3,256,512]{2,1,0:T(8,128)(2,1)} %param.31), kind=kLoop, calls=%fused_computation.39 | loop fusion | bytes 1572864 | tf_op jit(solution)/shard_map/slice | solution.py:236
  21.0 0.1 pad_add_fusion
  21.1 0.0 copy-done.26
  21.1 0.9 %multiply_add_fusion = s32[1,12288]{1,0:T(1,128)} fusion(s32[1,12288]{1,0:T(1,128)S(1)} %copy-done.26, s32[1,12288]{1,0:T(1,128)S(1)} %copy-done.27, pred[]{:T(512)S(6)} %eq.19, pred[]{:T(512)S(6)} %eq.23, pred[]{:T(512)S(6)} %eq.22), kind=kLoop, calls=%fused_computation.23 | loop fusion | flops 184320 | bytes 147459 | tf_op jit(solution)/shard_map/add | solution.py:260
  22.0 2.3 %sort.14 = (s32[96,128]{1,0:T(8,128)S(1)}, s32[96,128]{1,0:T(8,128)}) sort(s32[96,128]{1,0:T(8,128)} %bitcast.46, s32[96,128]{1,0:T(8,128)S(1)} %iota.9), dimensions={0}, to_apply=%region_0.1 | sort | flops 172032 | bytes 196608 | tf_op jit(solution)/shard_map/sort | solution.py:261
  24.3 0.1 fusion.halo_hot
  24.4 0.7 slice_reduce_fusion
  25.0 0.7 dynamic-slice_bitcast_fusion.1.out_mine
  25.7 0.0 copy-done.24
  25.7 1.0 %slice_bitcast_fusion.8 = (bf16[512,256]{1,0:T(8,128)(2,1)}, bf16[512,256]{1,0:T(8,128)(2,1)}, bf16[512,256]{1,0:T(8,128)(2,1)}, bf16[512,256]{1,0:T(8,128)(2,1)}) fusion(bf16[2,512,256]{2,1,0:T(8,128)(2,1)S(1)} %copy-done.23, bf16[2,512,256]{2,1,0:T(8,128)(2,1)S(1)} %copy-done.24), kind=kLoop, calls=%fused_computation.8 | loop fusion | bytes 2097152 | tf_op jit(solution)/shard_map/squeeze | solution.py:243
  26.7 1.4 %slice_convert_fusion.3 = (f32[1,256]{1,0:T(1,128)}, f32[1,256]{1,0:T(1,128)}, f32[1,256]{1,0:T(1,128)}, f32[1,256]{1,0:T(1,128)}, f32[1,256]{1,0:T(1,128)}) fusion(bf16[2,256]{1,0:T(2,128)(2,1)S(1)} %copy-done.30, bf16[3,256]{1,0:T(4,128)(2,1)} %param.30), kind=kLoop, calls=%fused_computation.27 | loop fusion | flops 1280 | bytes 7680 | tf_op jit(solution)/shard_map/convert_element_type | solution.py:243
  28.1 0.0 copy-done.22
  28.1 1.1 %slice_bitcast_fusion.3 = (bf16[1024,256]{1,0:T(8,128)(2,1)S(1)}, bf16[1024,256]{1,0:T(8,128)(2,1)}, bf16[1024,256]{1,0:T(8,128)(2,1)}) fusion(bf16[3,1024,256]{2,1,0:T(8,128)(2,1)S(1)} %copy-done.22), kind=kLoop, calls=%fused_computation.3 | loop fusion | bytes 3145728 | tf_op jit(solution)/shard_map/squeeze | solution.py:241
  29.2 0.0 copy-done.25
  29.2 2.0 %all_gather.3.state = bf16[256,512]{1,0:T(8,128)(2,1)S(1)} all-gather(bf16[256,256]{1,0:T(8,128)(2,1)S(1)} %copy-done.25), channel_id=1, replica_groups=mesh['band'=64,'feat'=2] {'feat'}, dimensions={1}, use_global_device_ids=true | all-gather | bytes 393216 | tf_op jit(solution)/shard_map/all_gather | solution.py:232
  31.2 0.0 copy-done.28
  31.2 0.1 reshape.36.node
  31.3 0.1 reshape.37.weight
  32.1 0.0 collective-permute-done.1
  32.1 1.4 %slice_convert_fusion = (f32[1,256]{1,0:T(1,128)}, f32[1,256]{1,0:T(1,128)}, f32[1,256]{1,0:T(1,128)}) fusion(bf16[3,256]{1,0:T(4,128)(2,1)} %collective-permute-done.1), kind=kLoop, calls=%fused_computation.24 | loop fusion | flops 768 | bytes 4608 | tf_op jit(solution)/shard_map/convert_element_type | solution.py:240
  33.4 0.0 collective-permute-done.2
  33.4 2.0 %fusion.4 = (bf16[1,256,512]{2,1,0:T(8,128)(2,1)S(1)}, bf16[256,512]{1,0:T(8,128)(2,1)}, bf16[256,512]{1,0:T(8,128)(2,1)}) fusion(bf16[3,256,512]{2,1,0:T(8,128)(2,1)} %collective-permute-done.2), kind=kLoop, calls=%fused_computation.38 | loop fusion | bytes 1572864 | tf_op jit(solution)/shard_map/slice | solution.py:236
  35.5 0.7 dynamic-slice_bitcast_fusion.out_other
  36.1 0.0 collective-permute-done
  36.1 2.4 %slice_bitcast_fusion = (bf16[1024,256]{1,0:T(8,128)(2,1)S(1)}, bf16[1024,256]{1,0:T(8,128)(2,1)}, bf16[1024,256]{1,0:T(8,128)(2,1)}) fusion(bf16[3,1024,256]{2,1,0:T(8,128)(2,1)} %collective-permute-done), kind=kLoop, calls=%fused_computation | loop fusion | bytes 3145728 | tf_op jit(solution)/shard_map/squeeze | solution.py:241
  38.5 7.4 %all-to-all-done = bf16[64,64,256]{2,1,0:T(8,128)(2,1)S(1)} async-done(((bf16[64,64,256]{2,1,0:T(8,128)(2,1)}), bf16[64,64,256]{2,1,0:T(8,128)(2,1)S(1)}, u32[]{:S(2)}, u32[]{:S(2)}) %all-to-all-start) | async-done | bytes 2097184 | tf_op jit(solution)/shard_map/all_to_all | solution.py:225
  46.0 0.7 slots.1.mine
  46.7 2.5 %collective-permute-start.3 = (bf16[256,256]{1,0:T(8,128)(2,1)S(1)}, bf16[256,256]{1,0:T(8,128)(2,1)S(1)}, u32[]{:S(2)}, u32[]{:S(2)}) collective-permute-start(bf16[256,256]{1,0:T(8,128)(2,1)S(1)} %slots.1.mine), channel_id=1, source_target_pairs={{0,1},{1,0},{2,3},{3,2},{4,5},{5,4},{6,7},{7,6},{8,9},{9,8},{10,11... | collective-permute-start | bytes 393224 | tf_op jit(solution)/shard_map/ppermute | solution.py:186
  49.2 0.0 copy-done.3
  49.2 0.4 own_terms.3
  49.6 0.6 collective-permute-done.3.other
  50.2 0.8 %node.2 = (bf16[256,512]{1,0:T(8,128)(2,1)S(1)}, bf16[256,256]{1,0:T(8,128)(2,1)S(1)}, bf16[64,256]{1,0:T(8,128)(2,1)S(1)}, bf16[64,256]{1,0:T(8,128)(2,1)S(1)}) custom-call(s32[1]{0:T(128)} %bitcast.core, bf16[256,512]{1,0:T(8,128)(2,1)S(1)} %all_gather.3.state, bf16[256,256]{1,0:T(8,128)(2,1)S(1)} %collective-permute-done.3.other, ...), custom_call_target="tpu_custom_call" | custom-call | flops 402653184 | bytes 1048576 | tf_op jit(solution)/shard_map/node/pallas_call | solution.py:302
  51.0 0.4 collective-permute-start.4
  51.5 0.5 collective-permute-start.5
  51.9 4.8 %edge_local.2 = (f32[256,12288]{1,0:T(8,128)S(1)}, f32[256,256]{1,0:T(8,128)S(1)}) custom-call(s32[1]{0:T(128)} %bitcast.21.few, s32[1,12288]{1,0:T(1,128)S(1)} %bitcast.42, bf16[256,256]{1,0:T(8,128)(2,1)S(1)} %get-tuple-element.85.sender, bf16[256,512]{1,0:T(8,128)(2,1)S(1)} %get-tuple-element.82.state, bf16[512,256]{1,0:T(8,128)(2,1)S(1)} %copy-done.13), custom_call_target="tpu_custom_call" | custom-call | flops 3221225472 | bytes 1048576 | tf_op jit(solution)/shard_map/edge_local/pallas_call | solution.py:311
  56.7 0.0 collective-permute-done.4.one
  56.7 0.0 collective-permute-done.5.two
  56.8 2.4 %edge_halo.2.mine = bf16[256,256]{1,0:T(8,128)(2,1)S(1)} custom-call(s32[1]{0:T(128)} %bitcast.21.few, s32[1,12288]{1,0:T(1,128)S(1)} %bitcast.43, f32[256,12288]{1,0:T(8,128)S(1)} %get-tuple-element.87.pre, f32[256,256]{1,0:T(8,128)S(1)} %get-tuple-element.88.partial, bf16[64,256]{1,0:T(8,128)(2,1)S(1)} %collective-permute-done.4.one, ...), custom_call_target="tpu_custom_call" | custom-call | flops 2415919104 | bytes 1048576 | tf_op jit(solution)/shard_map/edge_halo/pallas_call | solution.py:318
  59.2 1.0 %collective-permute-start.6 = (bf16[256,256]{1,0:T(8,128)(2,1)S(1)}, bf16[256,256]{1,0:T(8,128)(2,1)S(1)}, u32[]{:S(2)}, u32[]{:S(2)}) collective-permute-start(bf16[256,256]{1,0:T(8,128)(2,1)S(1)} %edge_halo.2.mine), channel_id=1, source_target_pairs={{0,1},{1,0},{2,3},{3,2},{4,5},{5,4},{6,7},{7,6},{8,9},{9,8},{10,11... | collective-permute-start | bytes 393224 | tf_op jit(solution)/shard_map/ppermute | solution.py:186
  60.2 0.0 copy-done
  60.2 0.0 copy-done.17
  60.2 0.4 own_terms.4
  60.6 0.6 collective-permute-done.6.other
  61.2 0.0 copy-done.4
  61.2 0.8 %node.3 = (bf16[256,512]{1,0:T(8,128)(2,1)S(1)}, bf16[256,256]{1,0:T(8,128)(2,1)S(1)}, bf16[64,256]{1,0:T(8,128)(2,1)S(1)}, bf16[64,256]{1,0:T(8,128)(2,1)S(1)}) custom-call(s32[1]{0:T(128)} %bitcast.core, bf16[256,512]{1,0:T(8,128)(2,1)S(1)} %get-tuple-element.82.state, bf16[256,256]{1,0:T(8,128)(2,1)S(1)} %collective-permute-done.6.other, ...), custom_call_target="tpu_custom_call" | custom-call | flops 402653184 | bytes 1048576 | tf_op jit(solution)/shard_map/node/pallas_call | solution.py:302
  62.0 0.4 collective-permute-start.7
  62.5 2.4 %collective-permute-start.8 = (bf16[64,256]{1,0:T(8,128)(2,1)S(1)}, bf16[64,256]{1,0:T(8,128)(2,1)S(1)}, u32[]{:S(2)}, u32[]{:S(2)}) collective-permute-start(bf16[64,256]{1,0:T(8,128)(2,1)S(1)} %get-tuple-element.107), channel_id=1, source_target_pairs={{0,2},{2,0},{4,6},{6,4},{8,10},{10,8},{12,14},{14,12},{16,18},{18,... | collective-permute-start | bytes 98312 | tf_op jit(solution)/shard_map/ppermute | solution.py:310
  64.8 4.8 %edge_local.3 = (f32[256,12288]{1,0:T(8,128)S(1)}, f32[256,256]{1,0:T(8,128)S(1)}) custom-call(s32[1]{0:T(128)} %bitcast.21.few, s32[1,12288]{1,0:T(1,128)S(1)} %bitcast.44, bf16[256,256]{1,0:T(8,128)(2,1)S(1)} %get-tuple-element.102.sender, bf16[256,512]{1,0:T(8,128)(2,1)S(1)} %get-tuple-element.101.state, bf16[512,256]{1,0:T(8,128)(2,1)S(1)} %copy-done.12), custom_call_target="tpu_custom_call" | custom-call | flops 3221225472 | bytes 1048576 | tf_op jit(solution)/shard_map/edge_local/pallas_call | solution.py:311
  69.7 0.0 collective-permute-done.7.one
  69.7 0.0 collective-permute-done.8.two
  69.7 0.0 copy-start.10
  69.7 2.4 %edge_halo.3.mine = bf16[256,256]{1,0:T(8,128)(2,1)S(1)} custom-call(s32[1]{0:T(128)} %bitcast.21.few, s32[1,12288]{1,0:T(1,128)S(1)} %bitcast.45, f32[256,12288]{1,0:T(8,128)S(1)} %get-tuple-element.104.pre, f32[256,256]{1,0:T(8,128)S(1)} %get-tuple-element.105.partial, bf16[64,256]{1,0:T(8,128)(2,1)S(1)} %collective-permute-done.7.one, ...), custom_call_target="tpu_custom_call" | custom-call | flops 2415919104 | bytes 1048576 | tf_op jit(solution)/shard_map/edge_halo/pallas_call | solution.py:318
  72.1 1.0 %collective-permute-start.9 = (bf16[256,256]{1,0:T(8,128)(2,1)S(1)}, bf16[256,256]{1,0:T(8,128)(2,1)S(1)}, u32[]{:S(2)}, u32[]{:S(2)}) collective-permute-start(bf16[256,256]{1,0:T(8,128)(2,1)S(1)} %edge_halo.3.mine), channel_id=1, source_target_pairs={{0,1},{1,0},{2,3},{3,2},{4,5},{5,4},{6,7},{7,6},{8,9},{9,8},{10,11... | collective-permute-start | bytes 393224 | tf_op jit(solution)/shard_map/ppermute | solution.py:186
  73.1 0.0 copy-done.19
  73.1 0.4 own_terms.5
  73.5 0.6 collective-permute-done.9.other
  74.1 1.1 %node_last.1 = bf16[256,256]{1,0:T(8,128)(2,1)} custom-call(s32[1]{0:T(128)} %bitcast.core, bf16[256,512]{1,0:T(8,128)(2,1)S(1)} %get-tuple-element.101.state, bf16[256,256]{1,0:T(8,128)(2,1)S(1)} %collective-permute-done.9.other, bf16[1024,256]{1,0:T(8,128)(2,1)S(1)} %get-tuple-element.108.in_mine, bf16[1024,256]{1,0:T(8,128)(2,1)S(1)} %get-tuple-element.109.in_other, ...), custom_call_target="tpu_custom_call" | custom-call | flops 402653184 | bytes 1048576 | tf_op jit(solution)/shard_map/node_last/pallas_call | solution.py:300
  (53 shorter events, 0.1 us)
Async XLA Ops:
  5.4 15.7 %copy-start.31 = (s32[1,2,64]{2,1,0:T(2,128)S(1)}, s32[1,2,64]{2,1,0:T(2,128)}, u32[]{:S(2)}) copy-start(s32[1,2,64]{2,1,0:T(2,128)} %param.25) | copy-start | bytes 1540
  5.4 15.8 %copy-start.26 = (s32[1,12288]{1,0:T(1,128)S(1)}, s32[1,12288]{1,0:T(1,128)}, u32[]{:S(2)}) copy-start(s32[1,12288]{1,0:T(1,128)} %param.24) | copy-start | bytes 147460
  5.4 15.8 %copy-start.27 = (s32[1,12288]{1,0:T(1,128)S(1)}, s32[1,12288]{1,0:T(1,128)}, u32[]{:S(2)}) copy-start(s32[1,12288]{1,0:T(1,128)} %param.23) | copy-start | bytes 147460
  5.4 40.6 %all-to-all-start = ((bf16[64,64,256]{2,1,0:T(8,128)(2,1)}), bf16[64,64,256]{2,1,0:T(8,128)(2,1)S(1)}, u32[]{:S(2)}, u32[]{:S(2)}) async-start(bf16[64,64,256]{2,1,0:T(8,128)(2,1)} %embed.1), calls=%async_computation | async-start | bytes 4194304 | tf_op jit(solution)/shard_map/all_to_all | solution.py:225
  17.5 8.2 %copy-start.23 = (bf16[2,512,256]{2,1,0:T(8,128)(2,1)S(1)}, bf16[2,512,256]{2,1,0:T(8,128)(2,1)}, u32[]{:S(2)}) copy-start(bf16[2,512,256]{2,1,0:T(8,128)(2,1)} %param.27) | copy-start | bytes 1572868
  17.5 8.2 %copy-start.24 = (bf16[2,512,256]{2,1,0:T(8,128)(2,1)S(1)}, bf16[2,512,256]{2,1,0:T(8,128)(2,1)}, u32[]{:S(2)}) copy-start(bf16[2,512,256]{2,1,0:T(8,128)(2,1)} %param.26) | copy-start | bytes 1572868
  17.5 14.6 %collective-permute-start.1 = (bf16[3,256]{1,0:T(4,128)(2,1)}, bf16[3,256]{1,0:T(4,128)(2,1)}, u32[]{:S(2)}, u32[]{:S(2)}) collective-permute-start(bf16[3,256]{1,0:T(4,128)(2,1)} %param.30), channel_id=1, source_target_pairs={{0,1},{1,0},{2,3},{3,2},{4,5},{5,4},{6,7},{7,6},{8,9},{9,8},{10,11... | collective-permute-start | bytes 4616 | tf_op jit(solution)/shard_map/ppermute | solution.py:186
  18.5 14.9 %collective-permute-start.2 = (bf16[3,256,512]{2,1,0:T(8,128)(2,1)}, bf16[3,256,512]{2,1,0:T(8,128)(2,1)}, u32[]{:S(2)}, u32[]{:S(2)}) collective-permute-start(bf16[3,256,512]{2,1,0:T(8,128)(2,1)} %param.31), channel_id=1, source_target_pairs={{0,1},{1,0},{2,3},{3,2},{4,5},{5,4},{6,7},{7,6},{8,9},{9,8},{10,11... | collective-permute-start | bytes 2359304 | tf_op jit(solution)/shard_map/ppermute | solution.py:186
  18.6 17.5 %collective-permute-start = (bf16[3,1024,256]{2,1,0:T(8,128)(2,1)}, bf16[3,1024,256]{2,1,0:T(8,128)(2,1)}, u32[]{:S(2)}, u32[]{:S(2)}) collective-permute-start(bf16[3,1024,256]{2,1,0:T(8,128)(2,1)} %param.29), channel_id=1, source_target_pairs={{0,1},{1,0},{2,3},{3,2},{4,5},{5,4},{6,7},{7,6},{8,9},{9,8},{10,11... | collective-permute-start | bytes 4718600 | tf_op jit(solution)/shard_map/ppermute | solution.py:186
  19.0 7.7 %copy-start.30 = (bf16[2,256]{1,0:T(2,128)(2,1)S(1)}, bf16[2,256]{1,0:T(2,128)(2,1)}, u32[]{:S(2)}) copy-start(bf16[2,256]{1,0:T(2,128)(2,1)} %param.28) | copy-start | bytes 3076
  25.0 3.1 %copy-start.22 = (bf16[3,1024,256]{2,1,0:T(8,128)(2,1)S(1)}, bf16[3,1024,256]{2,1,0:T(8,128)(2,1)}, u32[]{:S(2)}) copy-start(bf16[3,1024,256]{2,1,0:T(8,128)(2,1)} %param.29) | copy-start | bytes 4718596
  26.7 2.5 %copy-start.25 = (bf16[256,256]{1,0:T(8,128)(2,1)S(1)}, bf16[256,256]{1,0:T(8,128)(2,1)}, u32[]{:S(2)}) copy-start(bf16[256,256]{1,0:T(8,128)(2,1)} %param.17) | copy-start | bytes 393220
  26.7 4.5 %copy-start.28 = (s32[1,64,64]{2,1,0:T(8,128)S(1)}, s32[1,64,64]{2,1,0:T(8,128)}, u32[]{:S(2)}) copy-start(s32[1,64,64]{2,1,0:T(8,128)} %param.21) | copy-start | bytes 49156
  26.7 4.6 %copy-start.29 = (bf16[1,64,64]{2,1,0:T(8,128)(2,1)S(1)}, bf16[1,64,64]{2,1,0:T(8,128)(2,1)}, u32[]{:S(2)}) copy-start(bf16[1,64,64]{2,1,0:T(8,128)(2,1)} %param.22) | copy-start | bytes 24580
  45.9 3.3 %copy-start.2 = (bf16[1024,256]{1,0:T(8,128)(2,1)S(1)}, bf16[1024,256]{1,0:T(8,128)(2,1)}, u32[]{:S(2)}) copy-start(bf16[1024,256]{1,0:T(8,128)(2,1)} %get-tuple-element.71.in_mine) | copy-start | bytes 1572868
  45.9 3.3 %copy-start.3 = (bf16[1024,256]{1,0:T(8,128)(2,1)S(1)}, bf16[1024,256]{1,0:T(8,128)(2,1)}, u32[]{:S(2)}) copy-start(bf16[1024,256]{1,0:T(8,128)(2,1)} %get-tuple-element.72.in_other) | copy-start | bytes 1572868
  45.9 3.3 %copy-start.18 = (f32[1,256]{1,0:T(1,128)S(1)}, f32[1,256]{1,0:T(1,128)}, u32[]{:S(2)}) copy-start(f32[1,256]{1,0:T(1,128)} %get-tuple-element.73.bias_mine) | copy-start | bytes 3076
  45.9 3.3 %copy-start.21 = (f32[1,256]{1,0:T(1,128)S(1)}, f32[1,256]{1,0:T(1,128)}, u32[]{:S(2)}) copy-start(f32[1,256]{1,0:T(1,128)} %get-tuple-element.74.bias_other) | copy-start | bytes 3076
  45.9 4.3 %copy-start.5 = (bf16[256,512]{1,0:T(8,128)(2,1)S(1)}, bf16[256,512]{1,0:T(8,128)(2,1)}, u32[]{:S(2)}) copy-start(bf16[256,512]{1,0:T(8,128)(2,1)} %get-tuple-element.77.out_mine) | copy-start | bytes 786436
  45.9 4.3 %copy-start.7 = (bf16[256,512]{1,0:T(8,128)(2,1)S(1)}, bf16[256,512]{1,0:T(8,128)(2,1)}, u32[]{:S(2)}) copy-start(bf16[256,512]{1,0:T(8,128)(2,1)} %get-tuple-element.78.out_other) | copy-start | bytes 786436
  45.9 4.3 %copy-start.9 = (bf16[512,256]{1,0:T(8,128)(2,1)S(1)}, bf16[512,256]{1,0:T(8,128)(2,1)}, u32[]{:S(2)}) copy-start(bf16[512,256]{1,0:T(8,128)(2,1)} %get-tuple-element.79.send_w) | copy-start | bytes 786436
  46.0 4.3 %copy-start.15 = (f32[1,256]{1,0:T(1,128)S(1)}, f32[1,256]{1,0:T(1,128)}, u32[]{:S(2)}) copy-start(f32[1,256]{1,0:T(1,128)} %get-tuple-element.80.edge_bias) | copy-start | bytes 3076
  46.7 5.3 %copy-start.13 = (bf16[512,256]{1,0:T(8,128)(2,1)S(1)}, bf16[512,256]{1,0:T(8,128)(2,1)}, u32[]{:S(2)}) copy-start(bf16[512,256]{1,0:T(8,128)(2,1)} %get-tuple-element.86.recv_w) | copy-start | bytes 786436
  46.7 3.5 %collective-permute-start.3 = (bf16[256,256]{1,0:T(8,128)(2,1)S(1)}, bf16[256,256]{1,0:T(8,128)(2,1)S(1)}, u32[]{:S(2)}, u32[]{:S(2)}) collective-permute-start(bf16[256,256]{1,0:T(8,128)(2,1)S(1)} %slots.1.mine), channel_id=1, source_target_pairs={{0,1},{1,0},{2,3},{3,2},{4,5},{5,4},{6,7},{7,6},{8,9},{9,8},{10,11... | collective-permute-start | bytes 393224 | tf_op jit(solution)/shard_map/ppermute | solution.py:186
  51.0 5.7 %collective-permute-start.4 = (bf16[64,256]{1,0:T(8,128)(2,1)S(1)}, bf16[64,256]{1,0:T(8,128)(2,1)S(1)}, u32[]{:S(2)}, u32[]{:S(2)}) collective-permute-start(bf16[64,256]{1,0:T(8,128)(2,1)S(1)} %get-tuple-element.89), channel_id=1, source_target_pairs={{0,1},{1,0},{2,4},{3,5},{4,2},{5,3},{6,8},{7,9},{8,6},{9,7},{10,12... | collective-permute-start | bytes 98312 | tf_op jit(solution)/shard_map/ppermute | solution.py:309
  51.5 5.3 %collective-permute-start.5 = (bf16[64,256]{1,0:T(8,128)(2,1)S(1)}, bf16[64,256]{1,0:T(8,128)(2,1)S(1)}, u32[]{:S(2)}, u32[]{:S(2)}) collective-permute-start(bf16[64,256]{1,0:T(8,128)(2,1)S(1)} %get-tuple-element.90), channel_id=1, source_target_pairs={{0,2},{2,0},{4,6},{6,4},{8,10},{10,8},{12,14},{14,12},{16,18},{18,... | collective-permute-start | bytes 98312 | tf_op jit(solution)/shard_map/ppermute | solution.py:310
  56.8 3.5 %copy-start = (bf16[1024,256]{1,0:T(8,128)(2,1)S(1)}, bf16[1024,256]{1,0:T(8,128)(2,1)}, u32[]{:S(2)}) copy-start(bf16[1024,256]{1,0:T(8,128)(2,1)} %get-tuple-element.91.in_mine) | copy-start | bytes 1572868
  56.8 3.5 %copy-start.1 = (bf16[1024,256]{1,0:T(8,128)(2,1)S(1)}, bf16[1024,256]{1,0:T(8,128)(2,1)}, u32[]{:S(2)}) copy-start(bf16[1024,256]{1,0:T(8,128)(2,1)} %get-tuple-element.92.in_other) | copy-start | bytes 1572868
  56.8 3.5 %copy-start.17 = (f32[1,256]{1,0:T(1,128)S(1)}, f32[1,256]{1,0:T(1,128)}, u32[]{:S(2)}) copy-start(f32[1,256]{1,0:T(1,128)} %get-tuple-element.93.bias_mine) | copy-start | bytes 3076
  56.8 3.5 %copy-start.20 = (f32[1,256]{1,0:T(1,128)S(1)}, f32[1,256]{1,0:T(1,128)}, u32[]{:S(2)}) copy-start(f32[1,256]{1,0:T(1,128)} %get-tuple-element.94.bias_other) | copy-start | bytes 3076
  56.8 4.4 %copy-start.4 = (bf16[256,512]{1,0:T(8,128)(2,1)S(1)}, bf16[256,512]{1,0:T(8,128)(2,1)}, u32[]{:S(2)}) copy-start(bf16[256,512]{1,0:T(8,128)(2,1)} %get-tuple-element.97.out_mine) | copy-start | bytes 786436
  56.8 4.4 %copy-start.6 = (bf16[256,512]{1,0:T(8,128)(2,1)S(1)}, bf16[256,512]{1,0:T(8,128)(2,1)}, u32[]{:S(2)}) copy-start(bf16[256,512]{1,0:T(8,128)(2,1)} %get-tuple-element.98.out_other) | copy-start | bytes 786436
  56.8 4.4 %copy-start.8 = (bf16[512,256]{1,0:T(8,128)(2,1)S(1)}, bf16[512,256]{1,0:T(8,128)(2,1)}, u32[]{:S(2)}) copy-start(bf16[512,256]{1,0:T(8,128)(2,1)} %get-tuple-element.99.send_w) | copy-start | bytes 786436
  56.8 4.4 %copy-start.14 = (f32[1,256]{1,0:T(1,128)S(1)}, f32[1,256]{1,0:T(1,128)}, u32[]{:S(2)}) copy-start(f32[1,256]{1,0:T(1,128)} %get-tuple-element.100.edge_bias) | copy-start | bytes 3076
  59.2 5.6 %copy-start.12 = (bf16[512,256]{1,0:T(8,128)(2,1)S(1)}, bf16[512,256]{1,0:T(8,128)(2,1)}, u32[]{:S(2)}) copy-start(bf16[512,256]{1,0:T(8,128)(2,1)} %get-tuple-element.103.recv_w) | copy-start | bytes 786436
  59.2 2.0 %collective-permute-start.6 = (bf16[256,256]{1,0:T(8,128)(2,1)S(1)}, bf16[256,256]{1,0:T(8,128)(2,1)S(1)}, u32[]{:S(2)}, u32[]{:S(2)}) collective-permute-start(bf16[256,256]{1,0:T(8,128)(2,1)S(1)} %edge_halo.2.mine), channel_id=1, source_target_pairs={{0,1},{1,0},{2,3},{3,2},{4,5},{5,4},{6,7},{7,6},{8,9},{9,8},{10,11... | collective-permute-start | bytes 393224 | tf_op jit(solution)/shard_map/ppermute | solution.py:186
  62.0 7.6 %collective-permute-start.7 = (bf16[64,256]{1,0:T(8,128)(2,1)S(1)}, bf16[64,256]{1,0:T(8,128)(2,1)S(1)}, u32[]{:S(2)}, u32[]{:S(2)}) collective-permute-start(bf16[64,256]{1,0:T(8,128)(2,1)S(1)} %get-tuple-element.106), channel_id=1, source_target_pairs={{0,1},{1,0},{2,4},{3,5},{4,2},{5,3},{6,8},{7,9},{8,6},{9,7},{10,12... | collective-permute-start | bytes 98312 | tf_op jit(solution)/shard_map/ppermute | solution.py:309
  62.5 7.2 %collective-permute-start.8 = (bf16[64,256]{1,0:T(8,128)(2,1)S(1)}, bf16[64,256]{1,0:T(8,128)(2,1)S(1)}, u32[]{:S(2)}, u32[]{:S(2)}) collective-permute-start(bf16[64,256]{1,0:T(8,128)(2,1)S(1)} %get-tuple-element.107), channel_id=1, source_target_pairs={{0,2},{2,0},{4,6},{6,4},{8,10},{10,8},{12,14},{14,12},{16,18},{18,... | collective-permute-start | bytes 98312 | tf_op jit(solution)/shard_map/ppermute | solution.py:310
  69.7 3.4 %copy-start.16 = (f32[1,256]{1,0:T(1,128)S(1)}, f32[1,256]{1,0:T(1,128)}, u32[]{:S(2)}) copy-start(f32[1,256]{1,0:T(1,128)} %get-tuple-element.110.bias_mine) | copy-start | bytes 3076
  69.7 3.4 %copy-start.19 = (f32[1,256]{1,0:T(1,128)S(1)}, f32[1,256]{1,0:T(1,128)}, u32[]{:S(2)}) copy-start(f32[1,256]{1,0:T(1,128)} %get-tuple-element.111.bias_other) | copy-start | bytes 3076
  69.7 4.4 %copy-start.10 = (bf16[256,256]{1,0:T(8,128)(2,1)S(1)}, bf16[256,256]{1,0:T(8,128)(2,1)}, u32[]{:S(2)}) copy-start(bf16[256,256]{1,0:T(8,128)(2,1)} %dynamic-slice_bitcast_fusion.1.out_mine) | copy-start | bytes 393220
  69.7 4.4 %copy-start.11 = (bf16[256,256]{1,0:T(8,128)(2,1)S(1)}, bf16[256,256]{1,0:T(8,128)(2,1)}, u32[]{:S(2)}) copy-start(bf16[256,256]{1,0:T(8,128)(2,1)} %dynamic-slice_bitcast_fusion.out_other) | copy-start | bytes 393220
  72.1 2.0 %collective-permute-start.9 = (bf16[256,256]{1,0:T(8,128)(2,1)S(1)}, bf16[256,256]{1,0:T(8,128)(2,1)S(1)}, u32[]{:S(2)}, u32[]{:S(2)}) collective-permute-start(bf16[256,256]{1,0:T(8,128)(2,1)S(1)} %edge_halo.3.mine), channel_id=1, source_target_pairs={{0,1},{1,0},{2,3},{3,2},{4,5},{5,4},{6,7},{7,6},{8,9},{9,8},{10,11... | collective-permute-start | bytes 393224 | tf_op jit(solution)/shard_map/ppermute | solution.py:186
where the time goes:
time: 75.7 us; the launch traced here: 75.2 us
  Pallas kernels  24.2 us (32%)
  starting transfers between devices  21.9 us (29%)
  local copies, waits for them, and re-layouts  10.2 us (13%)
  waiting for transfers between devices  9.17 us (12%)
  other arithmetic  6.76 us (9%)
  blocking collectives  1.98 us (3%)
  between operations  1 us (1%)
    all_to_all x1, starting transfers between devices, body(): lax.all_to_all(outgoing, 'band', split_axis=0, concat_axis=0, tiled=True)  12.1 us
    pallas_call x2, Pallas kernels, body(): call(local_kernel, 'edge_local', (pltpu.VMEM((feature_width, edges), F32)...  9.59 us
    all_to_all x1, waiting for transfers between devices, body(): lax.all_to_all(outgoing, 'band', split_axis=0, concat_axis=0, tiled=True)  7.37 us
    ppermute x6, starting transfers between devices, swap_cores(): return lax.ppermute(value, 'feat', [(0, 1), (1, 0)])  6.1 us
    pallas_call x1, Pallas kernels, body(): call(embed_kernel, 'embed', jax.ShapeDtypeStruct((band_count, slot_count,...  5.35 us
    pallas_call x2, Pallas kernels, body(): call(halo_kernel, 'edge_halo', half, [SMEM] + [VMEM] * 5, 3 * edges * nod...  4.74 us
    slice x2, local copies, waits for them, and re-layouts, body(): out_w = [out_mine[layer], out_other[layer]]  3.98 us
    squeeze x2, local copies, waits for them, and re-layouts, body(): node_w.append((in_mine[layer], in_other[layer], *biases, *out_w))  3.54 us
  transfers between devices with their start and end apart: 11, of which 4 were waited for; matrix products, arithmetic and copies ran while one was open for 22% of the time, Pallas kernels for 14%

commit v1 on v0

--- a/solution.py
+++ b/solution.py
@@ -27,11 +27,11 @@
 
 
 LANES = 128
-BLOCK = 768
+BLOCK = 1024
 
 
 def head_of(edges):
-    return edges * 7 // 16 // BLOCK * BLOCK
+    return edges * 5 // 12 // BLOCK * BLOCK
 
 
 def over_blocks(edges, work):
@@ -47,35 +47,44 @@
     return jnp.where(ids == row.astype(jnp.int16), jnp.ones((), BF16), jnp.zeros((), BF16))
 
 
-def call(kernel, name, out_shape, in_specs, flops, limit=24, scratch=()):
+def call(kernel, name, out_shape, in_specs, flops, limit=24, scratch=(), out_specs=None):
     many = isinstance(out_shape, tuple)
     return pl.pallas_call(
         kernel,
         name=name,
         out_shape=out_shape,
         in_specs=in_specs,
-        out_specs=(VMEM,) * len(out_shape) if many else VMEM,
+        out_specs=out_specs or ((VMEM,) * len(out_shape) if many else VMEM),
         scratch_shapes=scratch,
         compiler_params=pltpu.CompilerParams(vmem_limit_bytes=limit * 2**20),
         cost_estimate=pl.CostEstimate(flops=flops, bytes_accessed=2**20, transcendentals=0),
     )
 
 
-def embed_kernel(grid, weights, bias, source, rows_out):
-    bands, slots, _ = rows_out.shape
+def embed_kernel(grid, weights, bias, source, rows_out, rows, sems):
+    bands, slots, _ = rows.shape
     count = grid.shape[0]
     add = bias[...].astype(F32).reshape(1, bias.shape[0])
     embedding = silu(dot32(grid[...], weights[...]) + add).astype(BF16)
     columns = source[0].T
     ids = lax.broadcasted_iota(jnp.int32, (slots, count), 1)
     group = 8 if bands % 8 == 0 else 1
-    for first in range(0, bands, group):
-        chosen = [
-            jnp.where(ids == columns[:, band : band + 1], jnp.ones((), BF16), jnp.zeros((), BF16))
-            for band in range(first, first + group)
-        ]
-        part = dot32(jnp.concatenate(chosen, 0), embedding).astype(BF16)
-        rows_out[first : first + group] = part.reshape(group, slots, part.shape[1])
+    ends = [bands // 2 // group * group, bands * 3 // 4 // group * group, bands]
+    copies = []
+    for first, end in zip([0, *ends[:-1]], ends):
+        for start in range(first, end, group):
+            chosen = [
+                jnp.where(ids == columns[:, i : i + 1], jnp.ones((), BF16), jnp.zeros((), BF16))
+                for i in range(start, start + group)
+            ]
+            part = dot32(jnp.concatenate(chosen, 0), embedding).astype(BF16)
+            rows[start : start + group] = part.reshape(group, slots, part.shape[1])
+        span = pl.ds(first, end - first)
+        copy = pltpu.make_async_copy(rows.at[span], rows_out.at[span], sems.at[len(copies)])
+        copy.start()
+        copies.append(copy)
+    for copy in copies:
+        copy.wait()
 
 
 def slots_kernel(node, weight, rows, aggregate):
@@ -221,6 +230,11 @@
         [VMEM] * 4,
         2 * slots * grid_latent.shape[0] * feature_width,
         limit=60,
+        scratch=[
+            pltpu.VMEM((band_count, slot_count, feature_width), BF16),
+            pltpu.SemaphoreType.DMA((3,)),
+        ],
+        out_specs=pl.BlockSpec(memory_space=pltpu.HBM),
     )(grid_latent, grid_in_w, grid_bias, g2m_src)
     incoming = lax.all_to_all(outgoing, "band", split_axis=0, concat_axis=0, tiled=True)
 

time: 75.7 us -> 75.7 us (level)
  transfers between devices with their start and end apart: 11 -> 11, of which waited for: 4 -> 4; matrix products, arithmetic and copies ran while one was open for 22% -> 22% of each run, Pallas kernels for 14% -> 15%
where the time goes in v1:
time: 75.7 us; the launch traced here: 75.2 us
  Pallas kernels  24.1 us (32%)
  starting transfers between devices  21.9 us (29%)
  local copies, waits for them, and re-layouts  10.2 us (13%)
  waiting for transfers between devices  9.17 us (12%)
  other arithmetic  6.76 us (9%)
  blocking collectives  1.98 us (3%)
  between operations  1.03 us (1%)
    all_to_all x1, starting transfers between devices, body(): lax.all_to_all(outgoing, 'band', split_axis=0, concat_axis=0, tiled=True)  12.1 us
    pallas_call x2, Pallas kernels, body(): call(local_kernel, 'edge_local', (pltpu.VMEM((feature_width, edges), F32)...  9.83 us
    all_to_all x1, waiting for transfers between devices, body(): lax.all_to_all(outgoing, 'band', split_axis=0, concat_axis=0, tiled=True)  7.37 us
    ppermute x6, starting transfers between devices, swap_cores(): return lax.ppermute(value, 'feat', [(0, 1), (1, 0)])  6.1 us
    pallas_call x2, Pallas kernels, body(): call(halo_kernel, 'edge_halo', half, [SMEM] + [VMEM] * 5, 3 * edges * nod...  4.9 us
    pallas_call x1, Pallas kernels, body(): call(embed_kernel, 'embed', jax.ShapeDtypeStruct((band_count, slot_count,...  4.86 us
    slice x2, local copies, waits for them, and re-layouts, body(): out_w = [out_mine[layer], out_other[layer]]  3.98 us
    squeeze x2, local copies, waits for them, and re-layouts, body(): node_w.append((in_mine[layer], in_other[layer], *biases, *out_w))  3.54 us
  transfers between devices with their start and end apart: 11, of which 4 were waited for; matrix products, arithmetic and copies ran while one was open for 22% of the time, Pallas kernels for 15%

profile of v1, /device:TPU:1, one launch (start us, length us, event | category | flops | bytes accessed | tf_op | source)
XLA Modules:
  0.0 75.2 jit_solution(17648596990259799915)
XLA Ops:
  0.0 4.9 %embed.1 = bf16[64,64,256]{2,1,0:T(8,128)(2,1)} custom-call(bf16[1024,512]{1,0:T(8,128)(2,1)} %grid.1, bf16[512,256]{1,0:T(8,128)(2,1)} %weights.1, bf16[256]{0:T(256)(128)(2,1)} %bias.1, s32[1,64,64]{2,1,0:T(8,128)} %source.1), custom_call_target="tpu_custom_call" | custom-call | flops 2147483648 | bytes 1048576 | tf_op jit(solution)/shard_map/embed/pallas_call | solution.py:226
  4.9 0.0 copy-start.31
  4.9 0.0 copy-start.26
  4.9 0.0 copy-start.27
  4.9 12.1 %all-to-all-start = ((bf16[64,64,256]{2,1,0:T(8,128)(2,1)}), bf16[64,64,256]{2,1,0:T(8,128)(2,1)S(1)}, u32[]{:S(2)}, u32[]{:S(2)}) async-start(bf16[64,64,256]{2,1,0:T(8,128)(2,1)} %embed.1), calls=%async_computation | async-start | bytes 4194304 | tf_op jit(solution)/shard_map/all_to_all | solution.py:239
  17.0 0.0 copy-start.23
  17.0 0.0 copy-start.24
  17.0 1.0 %collective-permute-start.1 = (bf16[3,256]{1,0:T(4,128)(2,1)}, bf16[3,256]{1,0:T(4,128)(2,1)}, u32[]{:S(2)}, u32[]{:S(2)}) collective-permute-start(bf16[3,256]{1,0:T(4,128)(2,1)} %param.30), channel_id=1, source_target_pairs={{0,1},{1,0},{2,3},{3,2},{4,5},{5,4},{6,7},{7,6},{8,9},{9,8},{10,11... | collective-permute-start | bytes 4616 | tf_op jit(solution)/shard_map/ppermute | solution.py:195
  18.1 0.1 collective-permute-start.2
  18.2 0.4 collective-permute-start
  18.6 2.0 %fusion.5 = (bf16[1,256,512]{2,1,0:T(8,128)(2,1)S(1)}, bf16[256,512]{1,0:T(8,128)(2,1)}, bf16[256,512]{1,0:T(8,128)(2,1)}) fusion(bf16[3,256,512]{2,1,0:T(8,128)(2,1)} %param.31), kind=kLoop, calls=%fused_computation.39 | loop fusion | bytes 1572864 | tf_op jit(solution)/shard_map/slice | solution.py:250
  20.6 0.1 pad_add_fusion
  20.7 0.0 copy-done.27
  20.7 0.9 %multiply_add_fusion = s32[1,12288]{1,0:T(1,128)} fusion(s32[1,12288]{1,0:T(1,128)S(1)} %copy-done.26, s32[1,12288]{1,0:T(1,128)S(1)} %copy-done.27, pred[]{:T(512)S(6)} %eq.19, pred[]{:T(512)S(6)} %eq.23, pred[]{:T(512)S(6)} %eq.22), kind=kLoop, calls=%fused_computation.23 | loop fusion | flops 184320 | bytes 147459 | tf_op jit(solution)/shard_map/add | solution.py:274
  21.5 2.3 %sort.14 = (s32[96,128]{1,0:T(8,128)S(1)}, s32[96,128]{1,0:T(8,128)}) sort(s32[96,128]{1,0:T(8,128)} %bitcast.46, s32[96,128]{1,0:T(8,128)S(1)} %iota.9), dimensions={0}, to_apply=%region_0.1 | sort | flops 172032 | bytes 196608 | tf_op jit(solution)/shard_map/sort | solution.py:275
  23.8 0.1 fusion.halo_hot
  23.9 0.7 slice_reduce_fusion
  24.6 0.7 dynamic-slice_bitcast_fusion.1.out_mine
  25.3 1.0 %slice_bitcast_fusion.8 = (bf16[512,256]{1,0:T(8,128)(2,1)}, bf16[512,256]{1,0:T(8,128)(2,1)}, bf16[512,256]{1,0:T(8,128)(2,1)}, bf16[512,256]{1,0:T(8,128)(2,1)}) fusion(bf16[2,512,256]{2,1,0:T(8,128)(2,1)S(1)} %copy-done.23, bf16[2,512,256]{2,1,0:T(8,128)(2,1)S(1)} %copy-done.24), kind=kLoop, calls=%fused_computation.8 | loop fusion | bytes 2097152 | tf_op jit(solution)/shard_map/squeeze | solution.py:257
  26.3 1.4 %slice_convert_fusion.3 = (f32[1,256]{1,0:T(1,128)}, f32[1,256]{1,0:T(1,128)}, f32[1,256]{1,0:T(1,128)}, f32[1,256]{1,0:T(1,128)}, f32[1,256]{1,0:T(1,128)}) fusion(bf16[2,256]{1,0:T(2,128)(2,1)S(1)} %copy-done.30, bf16[3,256]{1,0:T(4,128)(2,1)} %param.30), kind=kLoop, calls=%fused_computation.27 | loop fusion | flops 1280 | bytes 7680 | tf_op jit(solution)/shard_map/convert_element_type | solution.py:257
  27.7 1.1 %slice_bitcast_fusion.3 = (bf16[1024,256]{1,0:T(8,128)(2,1)S(1)}, bf16[1024,256]{1,0:T(8,128)(2,1)}, bf16[1024,256]{1,0:T(8,128)(2,1)}) fusion(bf16[3,1024,256]{2,1,0:T(8,128)(2,1)S(1)} %copy-done.22), kind=kLoop, calls=%fused_computation.3 | loop fusion | bytes 3145728 | tf_op jit(solution)/shard_map/squeeze | solution.py:255
  28.8 2.0 %all_gather.3.state = bf16[256,512]{1,0:T(8,128)(2,1)S(1)} all-gather(bf16[256,256]{1,0:T(8,128)(2,1)S(1)} %copy-done.25), channel_id=1, replica_groups=mesh['band'=64,'feat'=2] {'feat'}, dimensions={1}, use_global_device_ids=true | all-gather | bytes 393216 | tf_op jit(solution)/shard_map/all_gather | solution.py:246
  30.8 0.1 reshape.36.node
  30.9 0.0 copy-done.29
  30.9 0.1 reshape.37.weight
  31.6 0.0 collective-permute-done.1
  31.6 1.4 %slice_convert_fusion = (f32[1,256]{1,0:T(1,128)}, f32[1,256]{1,0:T(1,128)}, f32[1,256]{1,0:T(1,128)}) fusion(bf16[3,256]{1,0:T(4,128)(2,1)} %collective-permute-done.1), kind=kLoop, calls=%fused_computation.24 | loop fusion | flops 768 | bytes 4608 | tf_op jit(solution)/shard_map/convert_element_type | solution.py:254
  33.0 0.0 collective-permute-done.2
  33.0 2.0 %fusion.4 = (bf16[1,256,512]{2,1,0:T(8,128)(2,1)S(1)}, bf16[256,512]{1,0:T(8,128)(2,1)}, bf16[256,512]{1,0:T(8,128)(2,1)}) fusion(bf16[3,256,512]{2,1,0:T(8,128)(2,1)} %collective-permute-done.2), kind=kLoop, calls=%fused_computation.38 | loop fusion | bytes 1572864 | tf_op jit(solution)/shard_map/slice | solution.py:250
  35.0 0.7 dynamic-slice_bitcast_fusion.out_other
  35.7 0.0 collective-permute-done
  35.7 2.4 %slice_bitcast_fusion = (bf16[1024,256]{1,0:T(8,128)(2,1)S(1)}, bf16[1024,256]{1,0:T(8,128)(2,1)}, bf16[1024,256]{1,0:T(8,128)(2,1)}) fusion(bf16[3,1024,256]{2,1,0:T(8,128)(2,1)} %collective-permute-done), kind=kLoop, calls=%fused_computation | loop fusion | bytes 3145728 | tf_op jit(solution)/shard_map/squeeze | solution.py:255
  38.1 7.4 %all-to-all-done = bf16[64,64,256]{2,1,0:T(8,128)(2,1)S(1)} async-done(((bf16[64,64,256]{2,1,0:T(8,128)(2,1)}), bf16[64,64,256]{2,1,0:T(8,128)(2,1)S(1)}, u32[]{:S(2)}, u32[]{:S(2)}) %all-to-all-start) | async-done | bytes 2097184 | tf_op jit(solution)/shard_map/all_to_all | solution.py:239
  45.5 0.7 slots.1.mine
  46.2 2.5 %collective-permute-start.3 = (bf16[256,256]{1,0:T(8,128)(2,1)S(1)}, bf16[256,256]{1,0:T(8,128)(2,1)S(1)}, u32[]{:S(2)}, u32[]{:S(2)}) collective-permute-start(bf16[256,256]{1,0:T(8,128)(2,1)S(1)} %slots.1.mine), channel_id=1, source_target_pairs={{0,1},{1,0},{2,3},{3,2},{4,5},{5,4},{6,7},{7,6},{8,9},{9,8},{10,11... | collective-permute-start | bytes 393224 | tf_op jit(solution)/shard_map/ppermute | solution.py:195
  48.8 0.0 copy-done.2
  48.8 0.4 own_terms.3
  49.2 0.6 collective-permute-done.3.other
  49.8 0.0 copy-done.15
  49.8 0.8 %node.2 = (bf16[256,512]{1,0:T(8,128)(2,1)S(1)}, bf16[256,256]{1,0:T(8,128)(2,1)S(1)}, bf16[64,256]{1,0:T(8,128)(2,1)S(1)}, bf16[64,256]{1,0:T(8,128)(2,1)S(1)}) custom-call(s32[1]{0:T(128)} %bitcast.core, bf16[256,512]{1,0:T(8,128)(2,1)S(1)} %all_gather.3.state, bf16[256,256]{1,0:T(8,128)(2,1)S(1)} %collective-permute-done.3.other, ...), custom_call_target="tpu_custom_call" | custom-call | flops 402653184 | bytes 1048576 | tf_op jit(solution)/shard_map/node/pallas_call | solution.py:316
  50.6 0.5 collective-permute-start.4
  51.0 0.5 collective-permute-start.5
  51.5 4.9 %edge_local.2 = (f32[256,12288]{1,0:T(8,128)S(1)}, f32[256,256]{1,0:T(8,128)S(1)}) custom-call(s32[1]{0:T(128)} %bitcast.21.few, s32[1,12288]{1,0:T(1,128)S(1)} %bitcast.42, bf16[256,256]{1,0:T(8,128)(2,1)S(1)} %get-tuple-element.85.sender, bf16[256,512]{1,0:T(8,128)(2,1)S(1)} %get-tuple-element.82.state, bf16[512,256]{1,0:T(8,128)(2,1)S(1)} %copy-done.13), custom_call_target="tpu_custom_call" | custom-call | flops 3221225472 | bytes 1048576 | tf_op jit(solution)/shard_map/edge_local/pallas_call | solution.py:325
  56.4 0.0 collective-permute-done.4.one
  56.4 0.0 collective-permute-done.5.two
  56.4 0.0 copy-start
  56.4 0.0 copy-start.1
  56.4 0.0 copy-start.17
  56.5 2.5 %edge_halo.2.mine = bf16[256,256]{1,0:T(8,128)(2,1)S(1)} custom-call(s32[1]{0:T(128)} %bitcast.21.few, s32[1,12288]{1,0:T(1,128)S(1)} %bitcast.43, f32[256,12288]{1,0:T(8,128)S(1)} %get-tuple-element.87.pre, f32[256,256]{1,0:T(8,128)S(1)} %get-tuple-element.88.partial, bf16[64,256]{1,0:T(8,128)(2,1)S(1)} %collective-permute-done.4.one, ...), custom_call_target="tpu_custom_call" | custom-call | flops 2415919104 | bytes 1048576 | tf_op jit(solution)/shard_map/edge_halo/pallas_call | solution.py:332
  59.0 1.0 %collective-permute-start.6 = (bf16[256,256]{1,0:T(8,128)(2,1)S(1)}, bf16[256,256]{1,0:T(8,128)(2,1)S(1)}, u32[]{:S(2)}, u32[]{:S(2)}) collective-permute-start(bf16[256,256]{1,0:T(8,128)(2,1)S(1)} %edge_halo.2.mine), channel_id=1, source_target_pairs={{0,1},{1,0},{2,3},{3,2},{4,5},{5,4},{6,7},{7,6},{8,9},{9,8},{10,11... | collective-permute-start | bytes 393224 | tf_op jit(solution)/shard_map/ppermute | solution.py:195
  60.0 0.4 own_terms.4
  60.4 0.6 collective-permute-done.6.other
  61.0 0.8 %node.3 = (bf16[256,512]{1,0:T(8,128)(2,1)S(1)}, bf16[256,256]{1,0:T(8,128)(2,1)S(1)}, bf16[64,256]{1,0:T(8,128)(2,1)S(1)}, bf16[64,256]{1,0:T(8,128)(2,1)S(1)}) custom-call(s32[1]{0:T(128)} %bitcast.core, bf16[256,512]{1,0:T(8,128)(2,1)S(1)} %get-tuple-element.82.state, bf16[256,256]{1,0:T(8,128)(2,1)S(1)} %collective-permute-done.6.other, ...), custom_call_target="tpu_custom_call" | custom-call | flops 402653184 | bytes 1048576 | tf_op jit(solution)/shard_map/node/pallas_call | solution.py:316
  61.8 0.4 collective-permute-start.7
  62.2 2.4 %collective-permute-start.8 = (bf16[64,256]{1,0:T(8,128)(2,1)S(1)}, bf16[64,256]{1,0:T(8,128)(2,1)S(1)}, u32[]{:S(2)}, u32[]{:S(2)}) collective-permute-start(bf16[64,256]{1,0:T(8,128)(2,1)S(1)} %get-tuple-element.107), channel_id=1, source_target_pairs={{0,2},{2,0},{4,6},{6,4},{8,10},{10,8},{12,14},{14,12},{16,18},{18,... | collective-permute-start | bytes 98312 | tf_op jit(solution)/shard_map/ppermute | solution.py:324
  64.6 4.9 %edge_local.3 = (f32[256,12288]{1,0:T(8,128)S(1)}, f32[256,256]{1,0:T(8,128)S(1)}) custom-call(s32[1]{0:T(128)} %bitcast.21.few, s32[1,12288]{1,0:T(1,128)S(1)} %bitcast.44, bf16[256,256]{1,0:T(8,128)(2,1)S(1)} %get-tuple-element.102.sender, bf16[256,512]{1,0:T(8,128)(2,1)S(1)} %get-tuple-element.101.state, bf16[512,256]{1,0:T(8,128)(2,1)S(1)} %copy-done.12), custom_call_target="tpu_custom_call" | custom-call | flops 3221225472 | bytes 1048576 | tf_op jit(solution)/shard_map/edge_local/pallas_call | solution.py:325
  69.5 0.0 collective-permute-done.7.one
  69.5 0.0 collective-permute-done.8.two
  69.6 0.0 copy-start.10
  69.6 2.5 %edge_halo.3.mine = bf16[256,256]{1,0:T(8,128)(2,1)S(1)} custom-call(s32[1]{0:T(128)} %bitcast.21.few, s32[1,12288]{1,0:T(1,128)S(1)} %bitcast.45, f32[256,12288]{1,0:T(8,128)S(1)} %get-tuple-element.104.pre, f32[256,256]{1,0:T(8,128)S(1)} %get-tuple-element.105.partial, bf16[64,256]{1,0:T(8,128)(2,1)S(1)} %collective-permute-done.7.one, ...), custom_call_target="tpu_custom_call" | custom-call | flops 2415919104 | bytes 1048576 | tf_op jit(solution)/shard_map/edge_halo/pallas_call | solution.py:332
  72.0 1.0 %collective-permute-start.9 = (bf16[256,256]{1,0:T(8,128)(2,1)S(1)}, bf16[256,256]{1,0:T(8,128)(2,1)S(1)}, u32[]{:S(2)}, u32[]{:S(2)}) collective-permute-start(bf16[256,256]{1,0:T(8,128)(2,1)S(1)} %edge_halo.3.mine), channel_id=1, source_target_pairs={{0,1},{1,0},{2,3},{3,2},{4,5},{5,4},{6,7},{7,6},{8,9},{9,8},{10,11... | collective-permute-start | bytes 393224 | tf_op jit(solution)/shard_map/ppermute | solution.py:195
  73.1 0.4 own_terms.5
  73.4 0.6 collective-permute-done.9.other
  74.0 1.1 %node_last.1 = bf16[256,256]{1,0:T(8,128)(2,1)} custom-call(s32[1]{0:T(128)} %bitcast.core, bf16[256,512]{1,0:T(8,128)(2,1)S(1)} %get-tuple-element.101.state, bf16[256,256]{1,0:T(8,128)(2,1)S(1)} %collective-permute-done.9.other, bf16[1024,256]{1,0:T(8,128)(2,1)S(1)} %get-tuple-element.108.in_mine, bf16[1024,256]{1,0:T(8,128)(2,1)S(1)} %get-tuple-element.109.in_other, ...), custom_call_target="tpu_custom_call" | custom-call | flops 402653184 | bytes 1048576 | tf_op jit(solution)/shard_map/node_last/pallas_call | solution.py:314
  (53 shorter events, 0.1 us)
Async XLA Ops:
  4.9 15.7 %copy-start.31 = (s32[1,2,64]{2,1,0:T(2,128)S(1)}, s32[1,2,64]{2,1,0:T(2,128)}, u32[]{:S(2)}) copy-start(s32[1,2,64]{2,1,0:T(2,128)} %param.25) | copy-start | bytes 1540
  4.9 15.8 %copy-start.26 = (s32[1,12288]{1,0:T(1,128)S(1)}, s32[1,12288]{1,0:T(1,128)}, u32[]{:S(2)}) copy-start(s32[1,12288]{1,0:T(1,128)} %param.24) | copy-start | bytes 147460
  4.9 15.8 %copy-start.27 = (s32[1,12288]{1,0:T(1,128)S(1)}, s32[1,12288]{1,0:T(1,128)}, u32[]{:S(2)}) copy-start(s32[1,12288]{1,0:T(1,128)} %param.23) | copy-start | bytes 147460
  4.9 40.6 %all-to-all-start = ((bf16[64,64,256]{2,1,0:T(8,128)(2,1)}), bf16[64,64,256]{2,1,0:T(8,128)(2,1)S(1)}, u32[]{:S(2)}, u32[]{:S(2)}) async-start(bf16[64,64,256]{2,1,0:T(8,128)(2,1)} %embed.1), calls=%async_computation | async-start | bytes 4194304 | tf_op jit(solution)/shard_map/all_to_all | solution.py:239
  17.0 8.2 %copy-start.23 = (bf16[2,512,256]{2,1,0:T(8,128)(2,1)S(1)}, bf16[2,512,256]{2,1,0:T(8,128)(2,1)}, u32[]{:S(2)}) copy-start(bf16[2,512,256]{2,1,0:T(8,128)(2,1)} %param.27) | copy-start | bytes 1572868
  17.0 8.2 %copy-start.24 = (bf16[2,512,256]{2,1,0:T(8,128)(2,1)S(1)}, bf16[2,512,256]{2,1,0:T(8,128)(2,1)}, u32[]{:S(2)}) copy-start(bf16[2,512,256]{2,1,0:T(8,128)(2,1)} %param.26) | copy-start | bytes 1572868
  17.0 14.6 %collective-permute-start.1 = (bf16[3,256]{1,0:T(4,128)(2,1)}, bf16[3,256]{1,0:T(4,128)(2,1)}, u32[]{:S(2)}, u32[]{:S(2)}) collective-permute-start(bf16[3,256]{1,0:T(4,128)(2,1)} %param.30), channel_id=1, source_target_pairs={{0,1},{1,0},{2,3},{3,2},{4,5},{5,4},{6,7},{7,6},{8,9},{9,8},{10,11... | collective-permute-start | bytes 4616 | tf_op jit(solution)/shard_map/ppermute | solution.py:195
  18.1 14.9 %collective-permute-start.2 = (bf16[3,256,512]{2,1,0:T(8,128)(2,1)}, bf16[3,256,512]{2,1,0:T(8,128)(2,1)}, u32[]{:S(2)}, u32[]{:S(2)}) collective-permute-start(bf16[3,256,512]{2,1,0:T(8,128)(2,1)} %param.31), channel_id=1, source_target_pairs={{0,1},{1,0},{2,3},{3,2},{4,5},{5,4},{6,7},{7,6},{8,9},{9,8},{10,11... | collective-permute-start | bytes 2359304 | tf_op jit(solution)/shard_map/ppermute | solution.py:195
  18.2 17.5 %collective-permute-start = (bf16[3,1024,256]{2,1,0:T(8,128)(2,1)}, bf16[3,1024,256]{2,1,0:T(8,128)(2,1)}, u32[]{:S(2)}, u32[]{:S(2)}) collective-permute-start(bf16[3,1024,256]{2,1,0:T(8,128)(2,1)} %param.29), channel_id=1, source_target_pairs={{0,1},{1,0},{2,3},{3,2},{4,5},{5,4},{6,7},{7,6},{8,9},{9,8},{10,11... | collective-permute-start | bytes 4718600 | tf_op jit(solution)/shard_map/ppermute | solution.py:195
  18.6 7.7 %copy-start.30 = (bf16[2,256]{1,0:T(2,128)(2,1)S(1)}, bf16[2,256]{1,0:T(2,128)(2,1)}, u32[]{:S(2)}) copy-start(bf16[2,256]{1,0:T(2,128)(2,1)} %param.28) | copy-start | bytes 3076
  24.6 3.1 %copy-start.22 = (bf16[3,1024,256]{2,1,0:T(8,128)(2,1)S(1)}, bf16[3,1024,256]{2,1,0:T(8,128)(2,1)}, u32[]{:S(2)}) copy-start(bf16[3,1024,256]{2,1,0:T(8,128)(2,1)} %param.29) | copy-start | bytes 4718596
  26.3 2.5 %copy-start.25 = (bf16[256,256]{1,0:T(8,128)(2,1)S(1)}, bf16[256,256]{1,0:T(8,128)(2,1)}, u32[]{:S(2)}) copy-start(bf16[256,256]{1,0:T(8,128)(2,1)} %param.17) | copy-start | bytes 393220
  26.3 4.5 %copy-start.28 = (s32[1,64,64]{2,1,0:T(8,128)S(1)}, s32[1,64,64]{2,1,0:T(8,128)}, u32[]{:S(2)}) copy-start(s32[1,64,64]{2,1,0:T(8,128)} %param.21) | copy-start | bytes 49156
  26.3 4.6 %copy-start.29 = (bf16[1,64,64]{2,1,0:T(8,128)(2,1)S(1)}, bf16[1,64,64]{2,1,0:T(8,128)(2,1)}, u32[]{:S(2)}) copy-start(bf16[1,64,64]{2,1,0:T(8,128)(2,1)} %param.22) | copy-start | bytes 24580
  45.5 3.3 %copy-start.2 = (bf16[1024,256]{1,0:T(8,128)(2,1)S(1)}, bf16[1024,256]{1,0:T(8,128)(2,1)}, u32[]{:S(2)}) copy-start(bf16[1024,256]{1,0:T(8,128)(2,1)} %get-tuple-element.71.in_mine) | copy-start | bytes 1572868
  45.5 3.3 %copy-start.3 = (bf16[1024,256]{1,0:T(8,128)(2,1)S(1)}, bf16[1024,256]{1,0:T(8,128)(2,1)}, u32[]{:S(2)}) copy-start(bf16[1024,256]{1,0:T(8,128)(2,1)} %get-tuple-element.72.in_other) | copy-start | bytes 1572868
  45.5 3.3 %copy-start.18 = (f32[1,256]{1,0:T(1,128)S(1)}, f32[1,256]{1,0:T(1,128)}, u32[]{:S(2)}) copy-start(f32[1,256]{1,0:T(1,128)} %get-tuple-element.73.bias_mine) | copy-start | bytes 3076
  45.5 3.3 %copy-start.21 = (f32[1,256]{1,0:T(1,128)S(1)}, f32[1,256]{1,0:T(1,128)}, u32[]{:S(2)}) copy-start(f32[1,256]{1,0:T(1,128)} %get-tuple-element.74.bias_other) | copy-start | bytes 3076
  45.5 4.3 %copy-start.5 = (bf16[256,512]{1,0:T(8,128)(2,1)S(1)}, bf16[256,512]{1,0:T(8,128)(2,1)}, u32[]{:S(2)}) copy-start(bf16[256,512]{1,0:T(8,128)(2,1)} %get-tuple-element.77.out_mine) | copy-start | bytes 786436
  45.5 4.3 %copy-start.7 = (bf16[256,512]{1,0:T(8,128)(2,1)S(1)}, bf16[256,512]{1,0:T(8,128)(2,1)}, u32[]{:S(2)}) copy-start(bf16[256,512]{1,0:T(8,128)(2,1)} %get-tuple-element.78.out_other) | copy-start | bytes 786436
  45.5 4.3 %copy-start.9 = (bf16[512,256]{1,0:T(8,128)(2,1)S(1)}, bf16[512,256]{1,0:T(8,128)(2,1)}, u32[]{:S(2)}) copy-start(bf16[512,256]{1,0:T(8,128)(2,1)} %get-tuple-element.79.send_w) | copy-start | bytes 786436
  45.5 4.3 %copy-start.15 = (f32[1,256]{1,0:T(1,128)S(1)}, f32[1,256]{1,0:T(1,128)}, u32[]{:S(2)}) copy-start(f32[1,256]{1,0:T(1,128)} %get-tuple-element.80.edge_bias) | copy-start | bytes 3076
  46.2 5.3 %copy-start.13 = (bf16[512,256]{1,0:T(8,128)(2,1)S(1)}, bf16[512,256]{1,0:T(8,128)(2,1)}, u32[]{:S(2)}) copy-start(bf16[512,256]{1,0:T(8,128)(2,1)} %get-tuple-element.86.recv_w) | copy-start | bytes 786436
  46.2 3.5 %collective-permute-start.3 = (bf16[256,256]{1,0:T(8,128)(2,1)S(1)}, bf16[256,256]{1,0:T(8,128)(2,1)S(1)}, u32[]{:S(2)}, u32[]{:S(2)}) collective-permute-start(bf16[256,256]{1,0:T(8,128)(2,1)S(1)} %slots.1.mine), channel_id=1, source_target_pairs={{0,1},{1,0},{2,3},{3,2},{4,5},{5,4},{6,7},{7,6},{8,9},{9,8},{10,11... | collective-permute-start | bytes 393224 | tf_op jit(solution)/shard_map/ppermute | solution.py:195
  50.6 5.8 %collective-permute-start.4 = (bf16[64,256]{1,0:T(8,128)(2,1)S(1)}, bf16[64,256]{1,0:T(8,128)(2,1)S(1)}, u32[]{:S(2)}, u32[]{:S(2)}) collective-permute-start(bf16[64,256]{1,0:T(8,128)(2,1)S(1)} %get-tuple-element.89), channel_id=1, source_target_pairs={{0,1},{1,0},{2,4},{3,5},{4,2},{5,3},{6,8},{7,9},{8,6},{9,7},{10,12... | collective-permute-start | bytes 98312 | tf_op jit(solution)/shard_map/ppermute | solution.py:323
  51.0 5.4 %collective-permute-start.5 = (bf16[64,256]{1,0:T(8,128)(2,1)S(1)}, bf16[64,256]{1,0:T(8,128)(2,1)S(1)}, u32[]{:S(2)}, u32[]{:S(2)}) collective-permute-start(bf16[64,256]{1,0:T(8,128)(2,1)S(1)} %get-tuple-element.90), channel_id=1, source_target_pairs={{0,2},{2,0},{4,6},{6,4},{8,10},{10,8},{12,14},{14,12},{16,18},{18,... | collective-permute-start | bytes 98312 | tf_op jit(solution)/shard_map/ppermute | solution.py:324
  56.4 3.6 %copy-start = (bf16[1024,256]{1,0:T(8,128)(2,1)S(1)}, bf16[1024,256]{1,0:T(8,128)(2,1)}, u32[]{:S(2)}) copy-start(bf16[1024,256]{1,0:T(8,128)(2,1)} %get-tuple-element.91.in_mine) | copy-start | bytes 1572868
  56.4 3.5 %copy-start.1 = (bf16[1024,256]{1,0:T(8,128)(2,1)S(1)}, bf16[1024,256]{1,0:T(8,128)(2,1)}, u32[]{:S(2)}) copy-start(bf16[1024,256]{1,0:T(8,128)(2,1)} %get-tuple-element.92.in_other) | copy-start | bytes 1572868
  56.4 3.5 %copy-start.17 = (f32[1,256]{1,0:T(1,128)S(1)}, f32[1,256]{1,0:T(1,128)}, u32[]{:S(2)}) copy-start(f32[1,256]{1,0:T(1,128)} %get-tuple-element.93.bias_mine) | copy-start | bytes 3076
  56.5 3.5 %copy-start.20 = (f32[1,256]{1,0:T(1,128)S(1)}, f32[1,256]{1,0:T(1,128)}, u32[]{:S(2)}) copy-start(f32[1,256]{1,0:T(1,128)} %get-tuple-element.94.bias_other) | copy-start | bytes 3076
  56.5 4.5 %copy-start.4 = (bf16[256,512]{1,0:T(8,128)(2,1)S(1)}, bf16[256,512]{1,0:T(8,128)(2,1)}, u32[]{:S(2)}) copy-start(bf16[256,512]{1,0:T(8,128)(2,1)} %get-tuple-element.97.out_mine) | copy-start | bytes 786436
  56.5 4.5 %copy-start.6 = (bf16[256,512]{1,0:T(8,128)(2,1)S(1)}, bf16[256,512]{1,0:T(8,128)(2,1)}, u32[]{:S(2)}) copy-start(bf16[256,512]{1,0:T(8,128)(2,1)} %get-tuple-element.98.out_other) | copy-start | bytes 786436
  56.5 4.5 %copy-start.8 = (bf16[512,256]{1,0:T(8,128)(2,1)S(1)}, bf16[512,256]{1,0:T(8,128)(2,1)}, u32[]{:S(2)}) copy-start(bf16[512,256]{1,0:T(8,128)(2,1)} %get-tuple-element.99.send_w) | copy-start | bytes 786436
  56.5 4.5 %copy-start.14 = (f32[1,256]{1,0:T(1,128)S(1)}, f32[1,256]{1,0:T(1,128)}, u32[]{:S(2)}) copy-start(f32[1,256]{1,0:T(1,128)} %get-tuple-element.100.edge_bias) | copy-start | bytes 3076
  59.0 5.6 %copy-start.12 = (bf16[512,256]{1,0:T(8,128)(2,1)S(1)}, bf16[512,256]{1,0:T(8,128)(2,1)}, u32[]{:S(2)}) copy-start(bf16[512,256]{1,0:T(8,128)(2,1)} %get-tuple-element.103.recv_w) | copy-start | bytes 786436
  59.0 2.0 %collective-permute-start.6 = (bf16[256,256]{1,0:T(8,128)(2,1)S(1)}, bf16[256,256]{1,0:T(8,128)(2,1)S(1)}, u32[]{:S(2)}, u32[]{:S(2)}) collective-permute-start(bf16[256,256]{1,0:T(8,128)(2,1)S(1)} %edge_halo.2.mine), channel_id=1, source_target_pairs={{0,1},{1,0},{2,3},{3,2},{4,5},{5,4},{6,7},{7,6},{8,9},{9,8},{10,11... | collective-permute-start | bytes 393224 | tf_op jit(solution)/shard_map/ppermute | solution.py:195
  61.8 7.7 %collective-permute-start.7 = (bf16[64,256]{1,0:T(8,128)(2,1)S(1)}, bf16[64,256]{1,0:T(8,128)(2,1)S(1)}, u32[]{:S(2)}, u32[]{:S(2)}) collective-permute-start(bf16[64,256]{1,0:T(8,128)(2,1)S(1)} %get-tuple-element.106), channel_id=1, source_target_pairs={{0,1},{1,0},{2,4},{3,5},{4,2},{5,3},{6,8},{7,9},{8,6},{9,7},{10,12... | collective-permute-start | bytes 98312 | tf_op jit(solution)/shard_map/ppermute | solution.py:323
  62.2 7.3 %collective-permute-start.8 = (bf16[64,256]{1,0:T(8,128)(2,1)S(1)}, bf16[64,256]{1,0:T(8,128)(2,1)S(1)}, u32[]{:S(2)}, u32[]{:S(2)}) collective-permute-start(bf16[64,256]{1,0:T(8,128)(2,1)S(1)} %get-tuple-element.107), channel_id=1, source_target_pairs={{0,2},{2,0},{4,6},{6,4},{8,10},{10,8},{12,14},{14,12},{16,18},{18,... | collective-permute-start | bytes 98312 | tf_op jit(solution)/shard_map/ppermute | solution.py:324
  69.5 3.5 %copy-start.16 = (f32[1,256]{1,0:T(1,128)S(1)}, f32[1,256]{1,0:T(1,128)}, u32[]{:S(2)}) copy-start(f32[1,256]{1,0:T(1,128)} %get-tuple-element.110.bias_mine) | copy-start | bytes 3076
  69.6 3.5 %copy-start.19 = (f32[1,256]{1,0:T(1,128)S(1)}, f32[1,256]{1,0:T(1,128)}, u32[]{:S(2)}) copy-start(f32[1,256]{1,0:T(1,128)} %get-tuple-element.111.bias_other) | copy-start | bytes 3076
  69.6 4.5 %copy-start.10 = (bf16[256,256]{1,0:T(8,128)(2,1)S(1)}, bf16[256,256]{1,0:T(8,128)(2,1)}, u32[]{:S(2)}) copy-start(bf16[256,256]{1,0:T(8,128)(2,1)} %dynamic-slice_bitcast_fusion.1.out_mine) | copy-start | bytes 393220
  69.6 4.5 %copy-start.11 = (bf16[256,256]{1,0:T(8,128)(2,1)S(1)}, bf16[256,256]{1,0:T(8,128)(2,1)}, u32[]{:S(2)}) copy-start(bf16[256,256]{1,0:T(8,128)(2,1)} %dynamic-slice_bitcast_fusion.out_other) | copy-start | bytes 393220
  72.0 2.0 %collective-permute-start.9 = (bf16[256,256]{1,0:T(8,128)(2,1)S(1)}, bf16[256,256]{1,0:T(8,128)(2,1)S(1)}, u32[]{:S(2)}, u32[]{:S(2)}) collective-permute-start(bf16[256,256]{1,0:T(8,128)(2,1)S(1)} %edge_halo.3.mine), channel_id=1, source_target_pairs={{0,1},{1,0},{2,3},{3,2},{4,5},{5,4},{6,7},{7,6},{8,9},{9,8},{10,11... | collective-permute-start | bytes 393224 | tf_op jit(solution)/shard_map/ppermute | solution.py:195

commit v2 on v1

--- a/solution.py
+++ b/solution.py
@@ -27,11 +27,15 @@
 
 
 LANES = 128
-BLOCK = 1024
+BLOCK = 768
 
 
 def head_of(edges):
-    return edges * 5 // 12 // BLOCK * BLOCK
+    return edges * 5 // 8 // BLOCK * BLOCK
+
+
+def tail_of(edges):
+    return edges * 17 // 24 // (2 * LANES) * (2 * LANES)
 
 
 def over_blocks(edges, work):
@@ -137,10 +141,10 @@
     result[...] = (before.astype(F32) + update).astype(BF16)
 
 
-def local_kernel(few, keys, sender, state, recv_w, pre, partial):
+def local_kernel(usual, keys, sender, state, recv_w, pre, partial):
     nodes = sender.shape[0]
     shift = nodes.bit_length() - 1
-    head = head_of(keys.shape[1])
+    head, tail = head_of(keys.shape[1]), tail_of(keys.shape[1])
     receiver = dot32(state[...], recv_w[...]).astype(BF16)
     table = jnp.concatenate([sender[...].T, receiver.T], 1)
 
@@ -149,14 +153,16 @@
         chosen = jnp.concatenate([one_hot_columns(keys[:, edges] >> shift, nodes), to], 0)
         return dot32(table, chosen), to
 
-    @pl.when(few[0] == 1)
+    @pl.when(usual[0] == 1)
     def _():
         sums, to = gather(slice(0, head))
         messages = silu(sums).astype(BF16)
-        pre[:, head:] = gather(slice(head, None))[0]
+        pre[:, head:tail] = gather(slice(head, tail))[0]
+        receives = one_hot_columns(keys[:, tail:] & (nodes - 1), nodes)
+        pre[:, tail:] = dot32(table[:, nodes:], receives)
         partial[...] = dot32_nt(to, messages)
 
-    @pl.when(few[0] != 1)
+    @pl.when(usual[0] != 1)
     def _():
         def block(edges):
             pre[:, edges] = gather(edges)[0]
@@ -164,7 +170,7 @@
         over_blocks(keys.shape[1], block)
 
 
-def halo_kernel(few, keys, pre, partial, one, two, aggregate, total):
+def halo_kernel(usual, keys, pre, partial, one, two, aggregate, total):
     nodes = aggregate.shape[0]
     shift = nodes.bit_length() - 1
     head = head_of(keys.shape[1])
@@ -176,11 +182,11 @@
         to = one_hot_columns(keys[:, edges] & (nodes - 1), nodes)
         return dot32_nt(to, silu(sums).astype(BF16))
 
-    @pl.when(few[0] == 1)
+    @pl.when(usual[0] == 1)
     def _():
         total[...] = partial[...]
 
-    @pl.when(few[0] != 1)
+    @pl.when(usual[0] != 1)
     def _():
         def block(edges):
             total[...] += sums_of(edges)
@@ -271,15 +277,15 @@
     )
     outside = (from_previous & (part == 0)) | (from_next & (part == partitions - 1))
     source = jnp.where(outside, nodes + 2 * halo, source)
-    keys = (source * nodes + mesh_dst).reshape(edges // LANES, LANES)
-    keys = lax.sort(keys, dimension=0)
-    last = keys[head_of(edges) // LANES - 1]
-    few_halo = (jnp.max(last) < nodes * nodes).astype(jnp.int32).reshape(1)
+    keys = lax.sort((source * nodes + mesh_dst).reshape(edges), is_stable=False)
+    local = nodes * nodes
+    usual = (keys[head_of(edges) - 1] < local) & (keys[tail_of(edges)] >= local)
+    usual = usual.astype(jnp.int32).reshape(1)
     keys = keys.reshape(1, edges)
     slot_node, slot_weight = g2m_dst.reshape(1, slots), g2m_weight.reshape(1, slots)
-    incoming, core, state, node_w, edge_w, halo_hot, keys, few_halo, slot_node, slot_weight = (
+    incoming, core, state, node_w, edge_w, halo_hot, keys, usual, slot_node, slot_weight = (
         lax.optimization_barrier(
-            (incoming, core, state, node_w, edge_w, halo_hot, keys, few_halo, slot_node, slot_weight)
+            (incoming, core, state, node_w, edge_w, halo_hot, keys, usual, slot_node, slot_weight)
         )
     )
     half = jax.ShapeDtypeStruct((nodes, feature_width), BF16)
@@ -328,7 +334,7 @@
             (pltpu.VMEM((feature_width, edges), F32), total),
             [SMEM] + [VMEM] * 4,
             4 * edges * nodes * feature_width,
-        )(few_halo, keys, sender, state, recv_w)
+        )(usual, keys, sender, state, recv_w)
         aggregate = call(
             halo_kernel,
             "edge_halo",
@@ -336,7 +342,7 @@
             [SMEM] + [VMEM] * 5,
             3 * edges * nodes * feature_width,
             scratch=[pltpu.VMEM((nodes, feature_width), F32)],
-        )(few_halo, keys, pre, partial, arrived_one, arrived_two)
+        )(usual, keys, pre, partial, arrived_one, arrived_two)
 
 
 def solution(mesh):

time: 75.7 us -> 73.5 us (0.971)
  waiting for transfers between devices: 9.17 us -> 4.38 us
  other arithmetic: 6.76 us -> 10.3 us
  Pallas kernels: 24.1 us -> 22 us
    all_to_all x1, waiting for transfers between devices: 7.37 us -> 2.58 us  [body(): lax.all_to_all(outgoing, 'band', split_axis=0, concat_axis=0, tiled=True)]
    sort x1, other arithmetic: 2.29 us -> 6.3 us  [body(): keys = lax.sort((source * nodes + mesh_dst).reshape(edges), is_stable=False)]
    pallas_call x2, Pallas kernels: 4.9 us -> 3.5 us  [body(): call(halo_kernel, 'edge_halo', half, [SMEM] + [VMEM] * 5, 3 * edges * nod...]
  transfers between devices with their start and end apart: 11 -> 11, of which waited for: 4 -> 4; matrix products, arithmetic and copies ran while one was open for 22% -> 29% of each run, Pallas kernels for 15% -> 14%
where the time goes in v2:
time: 73.5 us; the launch traced here: 73 us
  Pallas kernels  22 us (30%)
  starting transfers between devices  21.9 us (30%)
  local copies, waits for them, and re-layouts  10.7 us (15%)
  other arithmetic  10.3 us (14%)
  waiting for transfers between devices  4.38 us (6%)
  blocking collectives  1.98 us (3%)
  between operations  1.7 us (2%)
    all_to_all x1, starting transfers between devices, body(): lax.all_to_all(outgoing, 'band', split_axis=0, concat_axis=0, tiled=True)  12.1 us
    pallas_call x2, Pallas kernels, body(): call(local_kernel, 'edge_local', (pltpu.VMEM((feature_width, edges), F32)...  9.12 us
    sort x1, other arithmetic, body(): keys = lax.sort((source * nodes + mesh_dst).reshape(edges), is_stable=False)  6.3 us
    ppermute x6, starting transfers between devices, swap_cores(): return lax.ppermute(value, 'feat', [(0, 1), (1, 0)])  6.11 us
    pallas_call x1, Pallas kernels, body(): call(embed_kernel, 'embed', jax.ShapeDtypeStruct((band_count, slot_count,...  4.84 us
    slice x2, local copies, waits for them, and re-layouts, body(): out_w = [out_mine[layer], out_other[layer]]  3.96 us
    squeeze x2, local copies, waits for them, and re-layouts, body(): node_w.append((in_mine[layer], in_other[layer], *biases, *out_w))  3.55 us
    pallas_call x2, Pallas kernels, body(): call(halo_kernel, 'edge_halo', half, [SMEM] + [VMEM] * 5, 3 * edges * nod...  3.5 us
  transfers between devices with their start and end apart: 11, of which 4 were waited for; matrix products, arithmetic and copies ran while one was open for 29% of the time, Pallas kernels for 14%

profile of v2, /device:TPU:1, one launch (start us, length us, event | category | flops | bytes accessed | tf_op | source)
XLA Modules:
  0.0 73.0 jit_solution(15773854946792877091)
XLA Ops:
  0.0 4.8 %embed.1 = bf16[64,64,256]{2,1,0:T(8,128)(2,1)} custom-call(bf16[1024,512]{1,0:T(8,128)(2,1)} %grid.1, bf16[512,256]{1,0:T(8,128)(2,1)} %weights.1, bf16[256]{0:T(256)(128)(2,1)} %bias.1, s32[1,64,64]{2,1,0:T(8,128)} %source.1), custom_call_target="tpu_custom_call" | custom-call | flops 2147483648 | bytes 1048576 | tf_op jit(solution)/shard_map/embed/pallas_call | solution.py:232
  4.8 0.0 copy-start.30
  4.9 0.0 copy-start.26
  4.9 12.1 %all-to-all-start = ((bf16[64,64,256]{2,1,0:T(8,128)(2,1)}), bf16[64,64,256]{2,1,0:T(8,128)(2,1)S(1)}, u32[]{:S(2)}, u32[]{:S(2)}) async-start(bf16[64,64,256]{2,1,0:T(8,128)(2,1)} %embed.1), calls=%async_computation | async-start | bytes 4194304 | tf_op jit(solution)/shard_map/all_to_all | solution.py:245
  17.0 0.0 copy-start.23
  17.0 0.0 copy-start.24
  17.0 1.0 %collective-permute-start.1 = (bf16[3,256]{1,0:T(4,128)(2,1)}, bf16[3,256]{1,0:T(4,128)(2,1)}, u32[]{:S(2)}, u32[]{:S(2)}) collective-permute-start(bf16[3,256]{1,0:T(4,128)(2,1)} %param.30), channel_id=1, source_target_pairs={{0,1},{1,0},{2,3},{3,2},{4,5},{5,4},{6,7},{7,6},{8,9},{9,8},{10,11... | collective-permute-start | bytes 4616 | tf_op jit(solution)/shard_map/ppermute | solution.py:201
  18.0 0.1 collective-permute-start.2
  18.1 0.4 collective-permute-start
  18.6 2.0 %fusion.5 = (bf16[1,256,512]{2,1,0:T(8,128)(2,1)S(1)}, bf16[256,512]{1,0:T(8,128)(2,1)}, bf16[256,512]{1,0:T(8,128)(2,1)}) fusion(bf16[3,256,512]{2,1,0:T(8,128)(2,1)} %param.31), kind=kLoop, calls=%fused_computation.38 | loop fusion | bytes 1572864 | tf_op jit(solution)/shard_map/slice | solution.py:256
  20.5 0.0 copy-done.30
  20.5 0.0 copy-done.26
  20.5 1.1 %multiply_add_fusion = s32[1,12288]{1,0:T(1,128)S(1)} fusion(s32[1,12288]{1,0:T(1,128)S(1)} %copy-done.26, s32[1,12288]{1,0:T(1,128)} %param.23, pred[]{:T(512)S(6)} %eq.19, pred[]{:T(512)S(6)} %eq.23, pred[]{:T(512)S(6)} %eq.22), kind=kLoop, calls=%fused_computation.23 | loop fusion | flops 184320 | bytes 147459 | tf_op jit(solution)/shard_map/add | solution.py:280
  21.6 6.3 %sort.7 = s32[12288]{0:T(1024)S(1)} sort(s32[12288]{0:T(1024)S(1)} %bitcast.45), dimensions={0}, to_apply=%region_0.1 | sort | flops 172032 | bytes 98304 | tf_op jit(solution)/shard_map/sort | solution.py:280
  27.9 0.1 pad_add_fusion
  28.0 0.1 fusion.halo_hot
  28.1 0.6 fusion.6
  28.7 0.7 dynamic-slice_bitcast_fusion.1.out_mine
  29.3 0.0 copy-done.24
  29.3 1.0 %slice_bitcast_fusion.8 = (bf16[512,256]{1,0:T(8,128)(2,1)}, bf16[512,256]{1,0:T(8,128)(2,1)}, bf16[512,256]{1,0:T(8,128)(2,1)}, bf16[512,256]{1,0:T(8,128)(2,1)}) fusion(bf16[2,512,256]{2,1,0:T(8,128)(2,1)S(1)} %copy-done.23, bf16[2,512,256]{2,1,0:T(8,128)(2,1)S(1)} %copy-done.24), kind=kLoop, calls=%fused_computation.8 | loop fusion | bytes 2097152 | tf_op jit(solution)/shard_map/squeeze | solution.py:263
  30.4 0.0 copy-done.29
  30.4 1.4 %slice_convert_fusion.3 = (f32[1,256]{1,0:T(1,128)}, f32[1,256]{1,0:T(1,128)}, f32[1,256]{1,0:T(1,128)}, f32[1,256]{1,0:T(1,128)}, f32[1,256]{1,0:T(1,128)}) fusion(bf16[2,256]{1,0:T(2,128)(2,1)S(1)} %copy-done.29, bf16[3,256]{1,0:T(4,128)(2,1)} %param.30), kind=kLoop, calls=%fused_computation.27 | loop fusion | flops 1280 | bytes 7680 | tf_op jit(solution)/shard_map/convert_element_type | solution.py:263
  31.8 1.1 %slice_bitcast_fusion.3 = (bf16[1024,256]{1,0:T(8,128)(2,1)S(1)}, bf16[1024,256]{1,0:T(8,128)(2,1)}, bf16[1024,256]{1,0:T(8,128)(2,1)}) fusion(bf16[3,1024,256]{2,1,0:T(8,128)(2,1)S(1)} %copy-done.22), kind=kLoop, calls=%fused_computation.3 | loop fusion | bytes 3145728 | tf_op jit(solution)/shard_map/squeeze | solution.py:261
  32.9 0.0 copy-done.25
  32.9 2.0 %all_gather.3.state = bf16[256,512]{1,0:T(8,128)(2,1)S(1)} all-gather(bf16[256,256]{1,0:T(8,128)(2,1)S(1)} %copy-done.25), channel_id=1, replica_groups=mesh['band'=64,'feat'=2] {'feat'}, dimensions={1}, use_global_device_ids=true | all-gather | bytes 393216 | tf_op jit(solution)/shard_map/all_gather | solution.py:252
  34.9 0.1 reshape.36.node
  35.0 0.1 reshape.37.weight
  36.4 0.0 collective-permute-done.1
  36.4 1.4 %slice_convert_fusion = (f32[1,256]{1,0:T(1,128)}, f32[1,256]{1,0:T(1,128)}, f32[1,256]{1,0:T(1,128)}) fusion(bf16[3,256]{1,0:T(4,128)(2,1)} %collective-permute-done.1), kind=kLoop, calls=%fused_computation.24 | loop fusion | flops 768 | bytes 4608 | tf_op jit(solution)/shard_map/convert_element_type | solution.py:260
  37.8 0.0 collective-permute-done.2
  37.8 2.0 %fusion.4 = (bf16[1,256,512]{2,1,0:T(8,128)(2,1)S(1)}, bf16[256,512]{1,0:T(8,128)(2,1)}, bf16[256,512]{1,0:T(8,128)(2,1)}) fusion(bf16[3,256,512]{2,1,0:T(8,128)(2,1)} %collective-permute-done.2), kind=kLoop, calls=%fused_computation.37 | loop fusion | bytes 1572864 | tf_op jit(solution)/shard_map/slice | solution.py:256
  39.7 0.7 dynamic-slice_bitcast_fusion.out_other
  40.4 0.0 collective-permute-done
  40.4 2.4 %slice_bitcast_fusion = (bf16[1024,256]{1,0:T(8,128)(2,1)S(1)}, bf16[1024,256]{1,0:T(8,128)(2,1)}, bf16[1024,256]{1,0:T(8,128)(2,1)}) fusion(bf16[3,1024,256]{2,1,0:T(8,128)(2,1)} %collective-permute-done), kind=kLoop, calls=%fused_computation | loop fusion | bytes 3145728 | tf_op jit(solution)/shard_map/squeeze | solution.py:261
  42.9 2.6 %all-to-all-done = bf16[64,64,256]{2,1,0:T(8,128)(2,1)S(1)} async-done(((bf16[64,64,256]{2,1,0:T(8,128)(2,1)}), bf16[64,64,256]{2,1,0:T(8,128)(2,1)S(1)}, u32[]{:S(2)}, u32[]{:S(2)}) %all-to-all-start) | async-done | bytes 2097184 | tf_op jit(solution)/shard_map/all_to_all | solution.py:245
  45.5 0.7 slots.1.mine
  46.2 2.5 %collective-permute-start.3 = (bf16[256,256]{1,0:T(8,128)(2,1)S(1)}, bf16[256,256]{1,0:T(8,128)(2,1)S(1)}, u32[]{:S(2)}, u32[]{:S(2)}) collective-permute-start(bf16[256,256]{1,0:T(8,128)(2,1)S(1)} %slots.1.mine), channel_id=1, source_target_pairs={{0,1},{1,0},{2,3},{3,2},{4,5},{5,4},{6,7},{7,6},{8,9},{9,8},{10,11... | collective-permute-start | bytes 393224 | tf_op jit(solution)/shard_map/ppermute | solution.py:201
  48.8 0.0 copy-done.2
  48.8 0.0 copy-done.18
  48.8 0.4 own_terms.3
  49.1 0.6 collective-permute-done.3.other
  49.7 0.0 copy-done.5
  49.8 0.8 %node.2 = (bf16[256,512]{1,0:T(8,128)(2,1)S(1)}, bf16[256,256]{1,0:T(8,128)(2,1)S(1)}, bf16[64,256]{1,0:T(8,128)(2,1)S(1)}, bf16[64,256]{1,0:T(8,128)(2,1)S(1)}) custom-call(s32[1]{0:T(128)} %bitcast.core, bf16[256,512]{1,0:T(8,128)(2,1)S(1)} %all_gather.3.state, bf16[256,256]{1,0:T(8,128)(2,1)S(1)} %collective-permute-done.3.other, ...), custom_call_target="tpu_custom_call" | custom-call | flops 402653184 | bytes 1048576 | tf_op jit(solution)/shard_map/node/pallas_call | solution.py:322
  50.5 0.4 collective-permute-start.4
  51.0 0.5 collective-permute-start.5
  51.5 4.5 %edge_local.2 = (f32[256,12288]{1,0:T(8,128)S(1)}, f32[256,256]{1,0:T(8,128)S(1)}) custom-call(s32[1]{0:T(128)S(6)} %convert_element_type.48.usual, s32[1,12288]{1,0:T(1,128)S(1)} %bitcast.41, bf16[256,256]{1,0:T(8,128)(2,1)S(1)} %get-tuple-element.82.sender, bf16[256,512]{1,0:T(8,128)(2,1)S(1)} %get-tuple-element.79.state, bf16[512,256]{1,0:T(8,128)(2,1)S(1)} %copy-done.13), custom_call_target="tpu_custom_call" | custom-call | flops 3221225472 | bytes 1048576 | tf_op jit(solution)/shard_map/edge_local/pallas_call | solution.py:331
  56.0 0.0 collective-permute-done.4.one
  56.0 0.0 collective-permute-done.5.two
  56.1 1.7 %edge_halo.2.mine = bf16[256,256]{1,0:T(8,128)(2,1)S(1)} custom-call(s32[1]{0:T(128)S(6)} %convert_element_type.48.usual, s32[1,12288]{1,0:T(1,128)S(1)} %bitcast.42, f32[256,12288]{1,0:T(8,128)S(1)} %get-tuple-element.84.pre, f32[256,256]{1,0:T(8,128)S(1)} %get-tuple-element.85.partial, bf16[64,256]{1,0:T(8,128)(2,1)S(1)} %collective-permute-done.4.one, ...), custom_call_target="tpu_custom_call" | custom-call | flops 2415919104 | bytes 1048576 | tf_op jit(solution)/shard_map/edge_halo/pallas_call | solution.py:338
  57.9 1.0 %collective-permute-start.6 = (bf16[256,256]{1,0:T(8,128)(2,1)S(1)}, bf16[256,256]{1,0:T(8,128)(2,1)S(1)}, u32[]{:S(2)}, u32[]{:S(2)}) collective-permute-start(bf16[256,256]{1,0:T(8,128)(2,1)S(1)} %edge_halo.2.mine), channel_id=1, source_target_pairs={{0,1},{1,0},{2,3},{3,2},{4,5},{5,4},{6,7},{7,6},{8,9},{9,8},{10,11... | collective-permute-start | bytes 393224 | tf_op jit(solution)/shard_map/ppermute | solution.py:201
  58.9 0.4 own_terms.4
  59.3 0.6 collective-permute-done.6.other
  59.9 0.8 %node.3 = (bf16[256,512]{1,0:T(8,128)(2,1)S(1)}, bf16[256,256]{1,0:T(8,128)(2,1)S(1)}, bf16[64,256]{1,0:T(8,128)(2,1)S(1)}, bf16[64,256]{1,0:T(8,128)(2,1)S(1)}) custom-call(s32[1]{0:T(128)} %bitcast.core, bf16[256,512]{1,0:T(8,128)(2,1)S(1)} %get-tuple-element.79.state, bf16[256,256]{1,0:T(8,128)(2,1)S(1)} %collective-permute-done.6.other, ...), custom_call_target="tpu_custom_call" | custom-call | flops 402653184 | bytes 1048576 | tf_op jit(solution)/shard_map/node/pallas_call | solution.py:322
  60.7 0.5 collective-permute-start.7
  61.1 2.4 %collective-permute-start.8 = (bf16[64,256]{1,0:T(8,128)(2,1)S(1)}, bf16[64,256]{1,0:T(8,128)(2,1)S(1)}, u32[]{:S(2)}, u32[]{:S(2)}) collective-permute-start(bf16[64,256]{1,0:T(8,128)(2,1)S(1)} %get-tuple-element.104), channel_id=1, source_target_pairs={{0,2},{2,0},{4,6},{6,4},{8,10},{10,8},{12,14},{14,12},{16,18},{18,... | collective-permute-start | bytes 98312 | tf_op jit(solution)/shard_map/ppermute | solution.py:330
  63.5 4.6 %edge_local.3 = (f32[256,12288]{1,0:T(8,128)S(1)}, f32[256,256]{1,0:T(8,128)S(1)}) custom-call(s32[1]{0:T(128)S(6)} %convert_element_type.48.usual, s32[1,12288]{1,0:T(1,128)S(1)} %bitcast.43, bf16[256,256]{1,0:T(8,128)(2,1)S(1)} %get-tuple-element.99.sender, bf16[256,512]{1,0:T(8,128)(2,1)S(1)} %get-tuple-element.98.state, bf16[512,256]{1,0:T(8,128)(2,1)S(1)} %copy-done.12), custom_call_target="tpu_custom_call" | custom-call | flops 3221225472 | bytes 1048576 | tf_op jit(solution)/shard_map/edge_local/pallas_call | solution.py:331
  68.1 0.0 collective-permute-done.7.one
  68.1 0.0 collective-permute-done.8.two
  68.1 0.0 copy-start.10
  68.1 1.8 %edge_halo.3.mine = bf16[256,256]{1,0:T(8,128)(2,1)S(1)} custom-call(s32[1]{0:T(128)S(6)} %convert_element_type.48.usual, s32[1,12288]{1,0:T(1,128)S(1)} %bitcast.44, f32[256,12288]{1,0:T(8,128)S(1)} %get-tuple-element.101.pre, f32[256,256]{1,0:T(8,128)S(1)} %get-tuple-element.102.partial, bf16[64,256]{1,0:T(8,128)(2,1)S(1)} %collective-permute-done.7.one, ...), custom_call_target="tpu_custom_call" | custom-call | flops 2415919104 | bytes 1048576 | tf_op jit(solution)/shard_map/edge_halo/pallas_call | solution.py:338
  69.9 1.0 %collective-permute-start.9 = (bf16[256,256]{1,0:T(8,128)(2,1)S(1)}, bf16[256,256]{1,0:T(8,128)(2,1)S(1)}, u32[]{:S(2)}, u32[]{:S(2)}) collective-permute-start(bf16[256,256]{1,0:T(8,128)(2,1)S(1)} %edge_halo.3.mine), channel_id=1, source_target_pairs={{0,1},{1,0},{2,3},{3,2},{4,5},{5,4},{6,7},{7,6},{8,9},{9,8},{10,11... | collective-permute-start | bytes 393224 | tf_op jit(solution)/shard_map/ppermute | solution.py:201
  70.9 0.4 own_terms.5
  71.3 0.6 collective-permute-done.9.other
  71.9 1.1 %node_last.1 = bf16[256,256]{1,0:T(8,128)(2,1)} custom-call(s32[1]{0:T(128)} %bitcast.core, bf16[256,512]{1,0:T(8,128)(2,1)S(1)} %get-tuple-element.98.state, bf16[256,256]{1,0:T(8,128)(2,1)S(1)} %collective-permute-done.9.other, bf16[1024,256]{1,0:T(8,128)(2,1)S(1)} %get-tuple-element.105.in_mine, bf16[1024,256]{1,0:T(8,128)(2,1)S(1)} %get-tuple-element.106.in_other, ...), custom_call_target="tpu_custom_call" | custom-call | flops 402653184 | bytes 1048576 | tf_op jit(solution)/shard_map/node_last/pallas_call | solution.py:320
  (50 shorter events, 0.1 us)
Async XLA Ops:
  4.8 15.7 %copy-start.30 = (s32[1,2,64]{2,1,0:T(2,128)S(1)}, s32[1,2,64]{2,1,0:T(2,128)}, u32[]{:S(2)}) copy-start(s32[1,2,64]{2,1,0:T(2,128)} %param.25) | copy-start | bytes 1540
  4.9 15.7 %copy-start.26 = (s32[1,12288]{1,0:T(1,128)S(1)}, s32[1,12288]{1,0:T(1,128)}, u32[]{:S(2)}) copy-start(s32[1,12288]{1,0:T(1,128)} %param.24) | copy-start | bytes 147460
  4.9 40.6 %all-to-all-start = ((bf16[64,64,256]{2,1,0:T(8,128)(2,1)}), bf16[64,64,256]{2,1,0:T(8,128)(2,1)S(1)}, u32[]{:S(2)}, u32[]{:S(2)}) async-start(bf16[64,64,256]{2,1,0:T(8,128)(2,1)} %embed.1), calls=%async_computation | async-start | bytes 4194304 | tf_op jit(solution)/shard_map/all_to_all | solution.py:245
  17.0 12.4 %copy-start.23 = (bf16[2,512,256]{2,1,0:T(8,128)(2,1)S(1)}, bf16[2,512,256]{2,1,0:T(8,128)(2,1)}, u32[]{:S(2)}) copy-start(bf16[2,512,256]{2,1,0:T(8,128)(2,1)} %param.27) | copy-start | bytes 1572868
  17.0 12.3 %copy-start.24 = (bf16[2,512,256]{2,1,0:T(8,128)(2,1)S(1)}, bf16[2,512,256]{2,1,0:T(8,128)(2,1)}, u32[]{:S(2)}) copy-start(bf16[2,512,256]{2,1,0:T(8,128)(2,1)} %param.26) | copy-start | bytes 1572868
  17.0 19.4 %collective-permute-start.1 = (bf16[3,256]{1,0:T(4,128)(2,1)}, bf16[3,256]{1,0:T(4,128)(2,1)}, u32[]{:S(2)}, u32[]{:S(2)}) collective-permute-start(bf16[3,256]{1,0:T(4,128)(2,1)} %param.30), channel_id=1, source_target_pairs={{0,1},{1,0},{2,3},{3,2},{4,5},{5,4},{6,7},{7,6},{8,9},{9,8},{10,11... | collective-permute-start | bytes 4616 | tf_op jit(solution)/shard_map/ppermute | solution.py:201
  18.0 19.7 %collective-permute-start.2 = (bf16[3,256,512]{2,1,0:T(8,128)(2,1)}, bf16[3,256,512]{2,1,0:T(8,128)(2,1)}, u32[]{:S(2)}, u32[]{:S(2)}) collective-permute-start(bf16[3,256,512]{2,1,0:T(8,128)(2,1)} %param.31), channel_id=1, source_target_pairs={{0,1},{1,0},{2,3},{3,2},{4,5},{5,4},{6,7},{7,6},{8,9},{9,8},{10,11... | collective-permute-start | bytes 2359304 | tf_op jit(solution)/shard_map/ppermute | solution.py:201
  18.1 22.3 %collective-permute-start = (bf16[3,1024,256]{2,1,0:T(8,128)(2,1)}, bf16[3,1024,256]{2,1,0:T(8,128)(2,1)}, u32[]{:S(2)}, u32[]{:S(2)}) collective-permute-start(bf16[3,1024,256]{2,1,0:T(8,128)(2,1)} %param.29), channel_id=1, source_target_pairs={{0,1},{1,0},{2,3},{3,2},{4,5},{5,4},{6,7},{7,6},{8,9},{9,8},{10,11... | collective-permute-start | bytes 4718600 | tf_op jit(solution)/shard_map/ppermute | solution.py:201
  18.6 11.8 %copy-start.29 = (bf16[2,256]{1,0:T(2,128)(2,1)S(1)}, bf16[2,256]{1,0:T(2,128)(2,1)}, u32[]{:S(2)}) copy-start(bf16[2,256]{1,0:T(2,128)(2,1)} %param.28) | copy-start | bytes 3076
  28.7 3.1 %copy-start.22 = (bf16[3,1024,256]{2,1,0:T(8,128)(2,1)S(1)}, bf16[3,1024,256]{2,1,0:T(8,128)(2,1)}, u32[]{:S(2)}) copy-start(bf16[3,1024,256]{2,1,0:T(8,128)(2,1)} %param.29) | copy-start | bytes 4718596
  30.4 2.5 %copy-start.25 = (bf16[256,256]{1,0:T(8,128)(2,1)S(1)}, bf16[256,256]{1,0:T(8,128)(2,1)}, u32[]{:S(2)}) copy-start(bf16[256,256]{1,0:T(8,128)(2,1)} %param.17) | copy-start | bytes 393220
  30.4 4.5 %copy-start.27 = (s32[1,64,64]{2,1,0:T(8,128)S(1)}, s32[1,64,64]{2,1,0:T(8,128)}, u32[]{:S(2)}) copy-start(s32[1,64,64]{2,1,0:T(8,128)} %param.21) | copy-start | bytes 49156
  30.4 4.6 %copy-start.28 = (bf16[1,64,64]{2,1,0:T(8,128)(2,1)S(1)}, bf16[1,64,64]{2,1,0:T(8,128)(2,1)}, u32[]{:S(2)}) copy-start(bf16[1,64,64]{2,1,0:T(8,128)(2,1)} %param.22) | copy-start | bytes 24580
  45.4 3.3 %copy-start.2 = (bf16[1024,256]{1,0:T(8,128)(2,1)S(1)}, bf16[1024,256]{1,0:T(8,128)(2,1)}, u32[]{:S(2)}) copy-start(bf16[1024,256]{1,0:T(8,128)(2,1)} %get-tuple-element.68.in_mine) | copy-start | bytes 1572868
  45.4 3.3 %copy-start.3 = (bf16[1024,256]{1,0:T(8,128)(2,1)S(1)}, bf16[1024,256]{1,0:T(8,128)(2,1)}, u32[]{:S(2)}) copy-start(bf16[1024,256]{1,0:T(8,128)(2,1)} %get-tuple-element.69.in_other) | copy-start | bytes 1572868
  45.4 3.3 %copy-start.18 = (f32[1,256]{1,0:T(1,128)S(1)}, f32[1,256]{1,0:T(1,128)}, u32[]{:S(2)}) copy-start(f32[1,256]{1,0:T(1,128)} %get-tuple-element.70.bias_mine) | copy-start | bytes 3076
  45.4 3.3 %copy-start.21 = (f32[1,256]{1,0:T(1,128)S(1)}, f32[1,256]{1,0:T(1,128)}, u32[]{:S(2)}) copy-start(f32[1,256]{1,0:T(1,128)} %get-tuple-element.71.bias_other) | copy-start | bytes 3076
  45.4 4.3 %copy-start.5 = (bf16[256,512]{1,0:T(8,128)(2,1)S(1)}, bf16[256,512]{1,0:T(8,128)(2,1)}, u32[]{:S(2)}) copy-start(bf16[256,512]{1,0:T(8,128)(2,1)} %get-tuple-element.74.out_mine) | copy-start | bytes 786436
  45.5 4.3 %copy-start.7 = (bf16[256,512]{1,0:T(8,128)(2,1)S(1)}, bf16[256,512]{1,0:T(8,128)(2,1)}, u32[]{:S(2)}) copy-start(bf16[256,512]{1,0:T(8,128)(2,1)} %get-tuple-element.75.out_other) | copy-start | bytes 786436
  45.5 4.3 %copy-start.9 = (bf16[512,256]{1,0:T(8,128)(2,1)S(1)}, bf16[512,256]{1,0:T(8,128)(2,1)}, u32[]{:S(2)}) copy-start(bf16[512,256]{1,0:T(8,128)(2,1)} %get-tuple-element.76.send_w) | copy-start | bytes 786436
  45.5 4.3 %copy-start.15 = (f32[1,256]{1,0:T(1,128)S(1)}, f32[1,256]{1,0:T(1,128)}, u32[]{:S(2)}) copy-start(f32[1,256]{1,0:T(1,128)} %get-tuple-element.77.edge_bias) | copy-start | bytes 3076
  46.2 5.3 %copy-start.13 = (bf16[512,256]{1,0:T(8,128)(2,1)S(1)}, bf16[512,256]{1,0:T(8,128)(2,1)}, u32[]{:S(2)}) copy-start(bf16[512,256]{1,0:T(8,128)(2,1)} %get-tuple-element.83.recv_w) | copy-start | bytes 786436
  46.2 3.5 %collective-permute-start.3 = (bf16[256,256]{1,0:T(8,128)(2,1)S(1)}, bf16[256,256]{1,0:T(8,128)(2,1)S(1)}, u32[]{:S(2)}, u32[]{:S(2)}) collective-permute-start(bf16[256,256]{1,0:T(8,128)(2,1)S(1)} %slots.1.mine), channel_id=1, source_target_pairs={{0,1},{1,0},{2,3},{3,2},{4,5},{5,4},{6,7},{7,6},{8,9},{9,8},{10,11... | collective-permute-start | bytes 393224 | tf_op jit(solution)/shard_map/ppermute | solution.py:201
  50.5 5.5 %collective-permute-start.4 = (bf16[64,256]{1,0:T(8,128)(2,1)S(1)}, bf16[64,256]{1,0:T(8,128)(2,1)S(1)}, u32[]{:S(2)}, u32[]{:S(2)}) collective-permute-start(bf16[64,256]{1,0:T(8,128)(2,1)S(1)} %get-tuple-element.86), channel_id=1, source_target_pairs={{0,1},{1,0},{2,4},{3,5},{4,2},{5,3},{6,8},{7,9},{8,6},{9,7},{10,12... | collective-permute-start | bytes 98312 | tf_op jit(solution)/shard_map/ppermute | solution.py:329
  51.0 5.0 %collective-permute-start.5 = (bf16[64,256]{1,0:T(8,128)(2,1)S(1)}, bf16[64,256]{1,0:T(8,128)(2,1)S(1)}, u32[]{:S(2)}, u32[]{:S(2)}) collective-permute-start(bf16[64,256]{1,0:T(8,128)(2,1)S(1)} %get-tuple-element.87), channel_id=1, source_target_pairs={{0,2},{2,0},{4,6},{6,4},{8,10},{10,8},{12,14},{14,12},{16,18},{18,... | collective-permute-start | bytes 98312 | tf_op jit(solution)/shard_map/ppermute | solution.py:330
  56.0 2.9 %copy-start = (bf16[1024,256]{1,0:T(8,128)(2,1)S(1)}, bf16[1024,256]{1,0:T(8,128)(2,1)}, u32[]{:S(2)}) copy-start(bf16[1024,256]{1,0:T(8,128)(2,1)} %get-tuple-element.88.in_mine) | copy-start | bytes 1572868
  56.0 2.8 %copy-start.1 = (bf16[1024,256]{1,0:T(8,128)(2,1)S(1)}, bf16[1024,256]{1,0:T(8,128)(2,1)}, u32[]{:S(2)}) copy-start(bf16[1024,256]{1,0:T(8,128)(2,1)} %get-tuple-element.89.in_other) | copy-start | bytes 1572868
  56.1 2.8 %copy-start.17 = (f32[1,256]{1,0:T(1,128)S(1)}, f32[1,256]{1,0:T(1,128)}, u32[]{:S(2)}) copy-start(f32[1,256]{1,0:T(1,128)} %get-tuple-element.90.bias_mine) | copy-start | bytes 3076
  56.1 2.8 %copy-start.20 = (f32[1,256]{1,0:T(1,128)S(1)}, f32[1,256]{1,0:T(1,128)}, u32[]{:S(2)}) copy-start(f32[1,256]{1,0:T(1,128)} %get-tuple-element.91.bias_other) | copy-start | bytes 3076
  56.1 3.8 %copy-start.4 = (bf16[256,512]{1,0:T(8,128)(2,1)S(1)}, bf16[256,512]{1,0:T(8,128)(2,1)}, u32[]{:S(2)}) copy-start(bf16[256,512]{1,0:T(8,128)(2,1)} %get-tuple-element.94.out_mine) | copy-start | bytes 786436
  56.1 3.8 %copy-start.6 = (bf16[256,512]{1,0:T(8,128)(2,1)S(1)}, bf16[256,512]{1,0:T(8,128)(2,1)}, u32[]{:S(2)}) copy-start(bf16[256,512]{1,0:T(8,128)(2,1)} %get-tuple-element.95.out_other) | copy-start | bytes 786436
  56.1 3.8 %copy-start.8 = (bf16[512,256]{1,0:T(8,128)(2,1)S(1)}, bf16[512,256]{1,0:T(8,128)(2,1)}, u32[]{:S(2)}) copy-start(bf16[512,256]{1,0:T(8,128)(2,1)} %get-tuple-element.96.send_w) | copy-start | bytes 786436
  56.1 3.8 %copy-start.14 = (f32[1,256]{1,0:T(1,128)S(1)}, f32[1,256]{1,0:T(1,128)}, u32[]{:S(2)}) copy-start(f32[1,256]{1,0:T(1,128)} %get-tuple-element.97.edge_bias) | copy-start | bytes 3076
  57.9 5.6 %copy-start.12 = (bf16[512,256]{1,0:T(8,128)(2,1)S(1)}, bf16[512,256]{1,0:T(8,128)(2,1)}, u32[]{:S(2)}) copy-start(bf16[512,256]{1,0:T(8,128)(2,1)} %get-tuple-element.100.recv_w) | copy-start | bytes 786436
  57.9 2.0 %collective-permute-start.6 = (bf16[256,256]{1,0:T(8,128)(2,1)S(1)}, bf16[256,256]{1,0:T(8,128)(2,1)S(1)}, u32[]{:S(2)}, u32[]{:S(2)}) collective-permute-start(bf16[256,256]{1,0:T(8,128)(2,1)S(1)} %edge_halo.2.mine), channel_id=1, source_target_pairs={{0,1},{1,0},{2,3},{3,2},{4,5},{5,4},{6,7},{7,6},{8,9},{9,8},{10,11... | collective-permute-start | bytes 393224 | tf_op jit(solution)/shard_map/ppermute | solution.py:201
  60.7 7.4 %collective-permute-start.7 = (bf16[64,256]{1,0:T(8,128)(2,1)S(1)}, bf16[64,256]{1,0:T(8,128)(2,1)S(1)}, u32[]{:S(2)}, u32[]{:S(2)}) collective-permute-start(bf16[64,256]{1,0:T(8,128)(2,1)S(1)} %get-tuple-element.103), channel_id=1, source_target_pairs={{0,1},{1,0},{2,4},{3,5},{4,2},{5,3},{6,8},{7,9},{8,6},{9,7},{10,12... | collective-permute-start | bytes 98312 | tf_op jit(solution)/shard_map/ppermute | solution.py:329
  61.1 7.0 %collective-permute-start.8 = (bf16[64,256]{1,0:T(8,128)(2,1)S(1)}, bf16[64,256]{1,0:T(8,128)(2,1)S(1)}, u32[]{:S(2)}, u32[]{:S(2)}) collective-permute-start(bf16[64,256]{1,0:T(8,128)(2,1)S(1)} %get-tuple-element.104), channel_id=1, source_target_pairs={{0,2},{2,0},{4,6},{6,4},{8,10},{10,8},{12,14},{14,12},{16,18},{18,... | collective-permute-start | bytes 98312 | tf_op jit(solution)/shard_map/ppermute | solution.py:330
  68.1 2.8 %copy-start.16 = (f32[1,256]{1,0:T(1,128)S(1)}, f32[1,256]{1,0:T(1,128)}, u32[]{:S(2)}) copy-start(f32[1,256]{1,0:T(1,128)} %get-tuple-element.107.bias_mine) | copy-start | bytes 3076
  68.1 2.8 %copy-start.19 = (f32[1,256]{1,0:T(1,128)S(1)}, f32[1,256]{1,0:T(1,128)}, u32[]{:S(2)}) copy-start(f32[1,256]{1,0:T(1,128)} %get-tuple-element.108.bias_other) | copy-start | bytes 3076
  68.1 3.8 %copy-start.10 = (bf16[256,256]{1,0:T(8,128)(2,1)S(1)}, bf16[256,256]{1,0:T(8,128)(2,1)}, u32[]{:S(2)}) copy-start(bf16[256,256]{1,0:T(8,128)(2,1)} %dynamic-slice_bitcast_fusion.1.out_mine) | copy-start | bytes 393220
  68.1 3.8 %copy-start.11 = (bf16[256,256]{1,0:T(8,128)(2,1)S(1)}, bf16[256,256]{1,0:T(8,128)(2,1)}, u32[]{:S(2)}) copy-start(bf16[256,256]{1,0:T(8,128)(2,1)} %dynamic-slice_bitcast_fusion.out_other) | copy-start | bytes 393220
  69.9 2.0 %collective-permute-start.9 = (bf16[256,256]{1,0:T(8,128)(2,1)S(1)}, bf16[256,256]{1,0:T(8,128)(2,1)S(1)}, u32[]{:S(2)}, u32[]{:S(2)}) collective-permute-start(bf16[256,256]{1,0:T(8,128)(2,1)S(1)} %edge_halo.3.mine), channel_id=1, source_target_pairs={{0,1},{1,0},{2,3},{3,2},{4,5},{5,4},{6,7},{7,6},{8,9},{9,8},{10,11... | collective-permute-start | bytes 393224 | tf_op jit(solution)/shard_map/ppermute | solution.py:201

commit v3 on v2

--- a/solution.py
+++ b/solution.py
@@ -27,15 +27,15 @@
 
 
 LANES = 128
-BLOCK = 768
+BLOCK = 256
 
 
 def head_of(edges):
-    return edges * 5 // 8 // BLOCK * BLOCK
+    return edges * 31 // 48 // BLOCK * BLOCK
 
 
 def tail_of(edges):
-    return edges * 17 // 24 // (2 * LANES) * (2 * LANES)
+    return edges * 11 // 16 // (2 * LANES) * (2 * LANES)
 
 
 def over_blocks(edges, work):

time: 73.5 us -> 73.3 us (level)
  no operation moved by 1% of the time
where the time goes in v3:
time: 73.3 us; the launch traced here: 72.7 us
  starting transfers between devices  22 us (30%)
  Pallas kernels  21.6 us (29%)
  local copies, waits for them, and re-layouts  10.7 us (15%)
  other arithmetic  10.3 us (14%)
  waiting for transfers between devices  4.38 us (6%)
  blocking collectives  1.98 us (3%)
  between operations  1.7 us (2%)
    all_to_all x1, starting transfers between devices, body(): lax.all_to_all(outgoing, 'band', split_axis=0, concat_axis=0, tiled=True)  12.1 us
    pallas_call x2, Pallas kernels, body(): call(local_kernel, 'edge_local', (pltpu.VMEM((feature_width, edges), F32)...  8.91 us
    sort x1, other arithmetic, body(): keys = lax.sort((source * nodes + mesh_dst).reshape(edges), is_stable=False)  6.3 us
    ppermute x6, starting transfers between devices, swap_cores(): return lax.ppermute(value, 'feat', [(0, 1), (1, 0)])  6.12 us
    pallas_call x1, Pallas kernels, body(): call(embed_kernel, 'embed', jax.ShapeDtypeStruct((band_count, slot_count,...  4.84 us
    slice x2, local copies, waits for them, and re-layouts, body(): out_w = [out_mine[layer], out_other[layer]]  3.96 us
    squeeze x2, local copies, waits for them, and re-layouts, body(): node_w.append((in_mine[layer], in_other[layer], *biases, *out_w))  3.55 us
    pallas_call x2, Pallas kernels, body(): call(halo_kernel, 'edge_halo', half, [SMEM] + [VMEM] * 5, 3 * edges * nod...  3.36 us
  transfers between devices with their start and end apart: 11, of which 4 were waited for; matrix products, arithmetic and copies ran while one was open for 29% of the time, Pallas kernels for 14%

profile of v3, /device:TPU:1, one launch (start us, length us, event | category | flops | bytes accessed | tf_op | source)
XLA Modules:
  0.0 72.7 jit_solution(5947959698881532923)
XLA Ops:
  0.0 4.8 %embed.1 = bf16[64,64,256]{2,1,0:T(8,128)(2,1)} custom-call(bf16[1024,512]{1,0:T(8,128)(2,1)} %grid.1, bf16[512,256]{1,0:T(8,128)(2,1)} %weights.1, bf16[256]{0:T(256)(128)(2,1)} %bias.1, s32[1,64,64]{2,1,0:T(8,128)} %source.1), custom_call_target="tpu_custom_call" | custom-call | flops 2147483648 | bytes 1048576 | tf_op jit(solution)/shard_map/embed/pallas_call | solution.py:232
  4.8 0.0 copy-start.30
  4.9 0.0 copy-start.26
  4.9 12.1 %all-to-all-start = ((bf16[64,64,256]{2,1,0:T(8,128)(2,1)}), bf16[64,64,256]{2,1,0:T(8,128)(2,1)S(1)}, u32[]{:S(2)}, u32[]{:S(2)}) async-start(bf16[64,64,256]{2,1,0:T(8,128)(2,1)} %embed.1), calls=%async_computation | async-start | bytes 4194304 | tf_op jit(solution)/shard_map/all_to_all | solution.py:245
  17.0 0.0 copy-start.23
  17.0 0.0 copy-start.24
  17.0 1.0 %collective-permute-start.1 = (bf16[3,256]{1,0:T(4,128)(2,1)}, bf16[3,256]{1,0:T(4,128)(2,1)}, u32[]{:S(2)}, u32[]{:S(2)}) collective-permute-start(bf16[3,256]{1,0:T(4,128)(2,1)} %param.30), channel_id=1, source_target_pairs={{0,1},{1,0},{2,3},{3,2},{4,5},{5,4},{6,7},{7,6},{8,9},{9,8},{10,11... | collective-permute-start | bytes 4616 | tf_op jit(solution)/shard_map/ppermute | solution.py:201
  18.0 0.1 collective-permute-start.2
  18.1 0.4 collective-permute-start
  18.6 2.0 %fusion.5 = (bf16[1,256,512]{2,1,0:T(8,128)(2,1)S(1)}, bf16[256,512]{1,0:T(8,128)(2,1)}, bf16[256,512]{1,0:T(8,128)(2,1)}) fusion(bf16[3,256,512]{2,1,0:T(8,128)(2,1)} %param.31), kind=kLoop, calls=%fused_computation.38 | loop fusion | bytes 1572864 | tf_op jit(solution)/shard_map/slice | solution.py:256
  20.5 1.1 %multiply_add_fusion = s32[1,12288]{1,0:T(1,128)S(1)} fusion(s32[1,12288]{1,0:T(1,128)S(1)} %copy-done.26, s32[1,12288]{1,0:T(1,128)} %param.23, pred[]{:T(512)S(6)} %eq.19, pred[]{:T(512)S(6)} %eq.23, pred[]{:T(512)S(6)} %eq.22), kind=kLoop, calls=%fused_computation.23 | loop fusion | flops 184320 | bytes 147459 | tf_op jit(solution)/shard_map/add | solution.py:280
  21.6 6.3 %sort.7 = s32[12288]{0:T(1024)S(1)} sort(s32[12288]{0:T(1024)S(1)} %bitcast.45), dimensions={0}, to_apply=%region_0.1 | sort | flops 172032 | bytes 98304 | tf_op jit(solution)/shard_map/sort | solution.py:280
  27.9 0.1 pad_add_fusion
  28.0 0.1 fusion.halo_hot
  28.1 0.6 fusion.6
  28.7 0.7 dynamic-slice_bitcast_fusion.1.out_mine
  29.3 1.0 %slice_bitcast_fusion.8 = (bf16[512,256]{1,0:T(8,128)(2,1)}, bf16[512,256]{1,0:T(8,128)(2,1)}, bf16[512,256]{1,0:T(8,128)(2,1)}, bf16[512,256]{1,0:T(8,128)(2,1)}) fusion(bf16[2,512,256]{2,1,0:T(8,128)(2,1)S(1)} %copy-done.23, bf16[2,512,256]{2,1,0:T(8,128)(2,1)S(1)} %copy-done.24), kind=kLoop, calls=%fused_computation.8 | loop fusion | bytes 2097152 | tf_op jit(solution)/shard_map/squeeze | solution.py:263
  30.4 1.4 %slice_convert_fusion.3 = (f32[1,256]{1,0:T(1,128)}, f32[1,256]{1,0:T(1,128)}, f32[1,256]{1,0:T(1,128)}, f32[1,256]{1,0:T(1,128)}, f32[1,256]{1,0:T(1,128)}) fusion(bf16[2,256]{1,0:T(2,128)(2,1)S(1)} %copy-done.29, bf16[3,256]{1,0:T(4,128)(2,1)} %param.30), kind=kLoop, calls=%fused_computation.27 | loop fusion | flops 1280 | bytes 7680 | tf_op jit(solution)/shard_map/convert_element_type | solution.py:263
  31.8 0.0 copy-done.22
  31.8 1.1 %slice_bitcast_fusion.3 = (bf16[1024,256]{1,0:T(8,128)(2,1)S(1)}, bf16[1024,256]{1,0:T(8,128)(2,1)}, bf16[1024,256]{1,0:T(8,128)(2,1)}) fusion(bf16[3,1024,256]{2,1,0:T(8,128)(2,1)S(1)} %copy-done.22), kind=kLoop, calls=%fused_computation.3 | loop fusion | bytes 3145728 | tf_op jit(solution)/shard_map/squeeze | solution.py:261
  32.9 2.0 %all_gather.3.state = bf16[256,512]{1,0:T(8,128)(2,1)S(1)} all-gather(bf16[256,256]{1,0:T(8,128)(2,1)S(1)} %copy-done.25), channel_id=1, replica_groups=mesh['band'=64,'feat'=2] {'feat'}, dimensions={1}, use_global_device_ids=true | all-gather | bytes 393216 | tf_op jit(solution)/shard_map/all_gather | solution.py:252
  34.9 0.0 copy-done.27
  34.9 0.1 reshape.36.node
  35.0 0.1 reshape.37.weight
  36.4 0.0 collective-permute-done.1
  36.4 1.4 %slice_convert_fusion = (f32[1,256]{1,0:T(1,128)}, f32[1,256]{1,0:T(1,128)}, f32[1,256]{1,0:T(1,128)}) fusion(bf16[3,256]{1,0:T(4,128)(2,1)} %collective-permute-done.1), kind=kLoop, calls=%fused_computation.24 | loop fusion | flops 768 | bytes 4608 | tf_op jit(solution)/shard_map/convert_element_type | solution.py:260
  37.8 0.0 collective-permute-done.2
  37.8 2.0 %fusion.4 = (bf16[1,256,512]{2,1,0:T(8,128)(2,1)S(1)}, bf16[256,512]{1,0:T(8,128)(2,1)}, bf16[256,512]{1,0:T(8,128)(2,1)}) fusion(bf16[3,256,512]{2,1,0:T(8,128)(2,1)} %collective-permute-done.2), kind=kLoop, calls=%fused_computation.37 | loop fusion | bytes 1572864 | tf_op jit(solution)/shard_map/slice | solution.py:256
  39.7 0.7 dynamic-slice_bitcast_fusion.out_other
  40.4 0.0 collective-permute-done
  40.4 2.4 %slice_bitcast_fusion = (bf16[1024,256]{1,0:T(8,128)(2,1)S(1)}, bf16[1024,256]{1,0:T(8,128)(2,1)}, bf16[1024,256]{1,0:T(8,128)(2,1)}) fusion(bf16[3,1024,256]{2,1,0:T(8,128)(2,1)} %collective-permute-done), kind=kLoop, calls=%fused_computation | loop fusion | bytes 3145728 | tf_op jit(solution)/shard_map/squeeze | solution.py:261
  42.9 2.6 %all-to-all-done = bf16[64,64,256]{2,1,0:T(8,128)(2,1)S(1)} async-done(((bf16[64,64,256]{2,1,0:T(8,128)(2,1)}), bf16[64,64,256]{2,1,0:T(8,128)(2,1)S(1)}, u32[]{:S(2)}, u32[]{:S(2)}) %all-to-all-start) | async-done | bytes 2097184 | tf_op jit(solution)/shard_map/all_to_all | solution.py:245
  45.4 0.0 copy-start.5
  45.5 0.0 copy-start.7
  45.5 0.0 copy-start.9
  45.5 0.0 copy-start.15
  45.5 0.7 slots.1.mine
  46.2 2.5 %collective-permute-start.3 = (bf16[256,256]{1,0:T(8,128)(2,1)S(1)}, bf16[256,256]{1,0:T(8,128)(2,1)S(1)}, u32[]{:S(2)}, u32[]{:S(2)}) collective-permute-start(bf16[256,256]{1,0:T(8,128)(2,1)S(1)} %slots.1.mine), channel_id=1, source_target_pairs={{0,1},{1,0},{2,3},{3,2},{4,5},{5,4},{6,7},{7,6},{8,9},{9,8},{10,11... | collective-permute-start | bytes 393224 | tf_op jit(solution)/shard_map/ppermute | solution.py:201
  48.8 0.0 copy-done.21
  48.8 0.4 own_terms.3
  49.1 0.6 collective-permute-done.3.other
  49.7 0.0 copy-done.7
  49.8 0.8 %node.2 = (bf16[256,512]{1,0:T(8,128)(2,1)S(1)}, bf16[256,256]{1,0:T(8,128)(2,1)S(1)}, bf16[64,256]{1,0:T(8,128)(2,1)S(1)}, bf16[64,256]{1,0:T(8,128)(2,1)S(1)}) custom-call(s32[1]{0:T(128)} %bitcast.core, bf16[256,512]{1,0:T(8,128)(2,1)S(1)} %all_gather.3.state, bf16[256,256]{1,0:T(8,128)(2,1)S(1)} %collective-permute-done.3.other, ...), custom_call_target="tpu_custom_call" | custom-call | flops 402653184 | bytes 1048576 | tf_op jit(solution)/shard_map/node/pallas_call | solution.py:322
  50.5 0.4 collective-permute-start.4
  51.0 0.5 collective-permute-start.5
  51.5 4.5 %edge_local.2 = (f32[256,12288]{1,0:T(8,128)S(1)}, f32[256,256]{1,0:T(8,128)S(1)}) custom-call(s32[1]{0:T(128)S(6)} %convert_element_type.48.usual, s32[1,12288]{1,0:T(1,128)S(1)} %bitcast.41, bf16[256,256]{1,0:T(8,128)(2,1)S(1)} %get-tuple-element.82.sender, bf16[256,512]{1,0:T(8,128)(2,1)S(1)} %get-tuple-element.79.state, bf16[512,256]{1,0:T(8,128)(2,1)S(1)} %copy-done.13), custom_call_target="tpu_custom_call" | custom-call | flops 3221225472 | bytes 1048576 | tf_op jit(solution)/shard_map/edge_local/pallas_call | solution.py:331
  56.0 0.0 collective-permute-done.4.one
  56.0 0.0 collective-permute-done.5.two
  56.1 1.7 %edge_halo.2.mine = bf16[256,256]{1,0:T(8,128)(2,1)S(1)} custom-call(s32[1]{0:T(128)S(6)} %convert_element_type.48.usual, s32[1,12288]{1,0:T(1,128)S(1)} %bitcast.42, f32[256,12288]{1,0:T(8,128)S(1)} %get-tuple-element.84.pre, f32[256,256]{1,0:T(8,128)S(1)} %get-tuple-element.85.partial, bf16[64,256]{1,0:T(8,128)(2,1)S(1)} %collective-permute-done.4.one, ...), custom_call_target="tpu_custom_call" | custom-call | flops 2415919104 | bytes 1048576 | tf_op jit(solution)/shard_map/edge_halo/pallas_call | solution.py:338
  57.8 1.0 %collective-permute-start.6 = (bf16[256,256]{1,0:T(8,128)(2,1)S(1)}, bf16[256,256]{1,0:T(8,128)(2,1)S(1)}, u32[]{:S(2)}, u32[]{:S(2)}) collective-permute-start(bf16[256,256]{1,0:T(8,128)(2,1)S(1)} %edge_halo.2.mine), channel_id=1, source_target_pairs={{0,1},{1,0},{2,3},{3,2},{4,5},{5,4},{6,7},{7,6},{8,9},{9,8},{10,11... | collective-permute-start | bytes 393224 | tf_op jit(solution)/shard_map/ppermute | solution.py:201
  58.8 0.4 own_terms.4
  59.2 0.6 collective-permute-done.6.other
  59.8 0.8 %node.3 = (bf16[256,512]{1,0:T(8,128)(2,1)S(1)}, bf16[256,256]{1,0:T(8,128)(2,1)S(1)}, bf16[64,256]{1,0:T(8,128)(2,1)S(1)}, bf16[64,256]{1,0:T(8,128)(2,1)S(1)}) custom-call(s32[1]{0:T(128)} %bitcast.core, bf16[256,512]{1,0:T(8,128)(2,1)S(1)} %get-tuple-element.79.state, bf16[256,256]{1,0:T(8,128)(2,1)S(1)} %collective-permute-done.6.other, ...), custom_call_target="tpu_custom_call" | custom-call | flops 402653184 | bytes 1048576 | tf_op jit(solution)/shard_map/node/pallas_call | solution.py:322
  60.6 0.5 collective-permute-start.7
  61.1 2.4 %collective-permute-start.8 = (bf16[64,256]{1,0:T(8,128)(2,1)S(1)}, bf16[64,256]{1,0:T(8,128)(2,1)S(1)}, u32[]{:S(2)}, u32[]{:S(2)}) collective-permute-start(bf16[64,256]{1,0:T(8,128)(2,1)S(1)} %get-tuple-element.104), channel_id=1, source_target_pairs={{0,2},{2,0},{4,6},{6,4},{8,10},{10,8},{12,14},{14,12},{16,18},{18,... | collective-permute-start | bytes 98312 | tf_op jit(solution)/shard_map/ppermute | solution.py:330
  63.4 4.4 %edge_local.3 = (f32[256,12288]{1,0:T(8,128)S(1)}, f32[256,256]{1,0:T(8,128)S(1)}) custom-call(s32[1]{0:T(128)S(6)} %convert_element_type.48.usual, s32[1,12288]{1,0:T(1,128)S(1)} %bitcast.43, bf16[256,256]{1,0:T(8,128)(2,1)S(1)} %get-tuple-element.99.sender, bf16[256,512]{1,0:T(8,128)(2,1)S(1)} %get-tuple-element.98.state, bf16[512,256]{1,0:T(8,128)(2,1)S(1)} %copy-done.12), custom_call_target="tpu_custom_call" | custom-call | flops 3221225472 | bytes 1048576 | tf_op jit(solution)/shard_map/edge_local/pallas_call | solution.py:331
  67.8 0.0 collective-permute-done.7.one
  67.8 0.0 collective-permute-done.8.two
  67.8 0.0 copy-start.10
  67.9 1.7 %edge_halo.3.mine = bf16[256,256]{1,0:T(8,128)(2,1)S(1)} custom-call(s32[1]{0:T(128)S(6)} %convert_element_type.48.usual, s32[1,12288]{1,0:T(1,128)S(1)} %bitcast.44, f32[256,12288]{1,0:T(8,128)S(1)} %get-tuple-element.101.pre, f32[256,256]{1,0:T(8,128)S(1)} %get-tuple-element.102.partial, bf16[64,256]{1,0:T(8,128)(2,1)S(1)} %collective-permute-done.7.one, ...), custom_call_target="tpu_custom_call" | custom-call | flops 2415919104 | bytes 1048576 | tf_op jit(solution)/shard_map/edge_halo/pallas_call | solution.py:338
  69.6 1.0 %collective-permute-start.9 = (bf16[256,256]{1,0:T(8,128)(2,1)S(1)}, bf16[256,256]{1,0:T(8,128)(2,1)S(1)}, u32[]{:S(2)}, u32[]{:S(2)}) collective-permute-start(bf16[256,256]{1,0:T(8,128)(2,1)S(1)} %edge_halo.3.mine), channel_id=1, source_target_pairs={{0,1},{1,0},{2,3},{3,2},{4,5},{5,4},{6,7},{7,6},{8,9},{9,8},{10,11... | collective-permute-start | bytes 393224 | tf_op jit(solution)/shard_map/ppermute | solution.py:201
  70.6 0.4 own_terms.5
  71.0 0.6 collective-permute-done.9.other
  71.6 1.1 %node_last.1 = bf16[256,256]{1,0:T(8,128)(2,1)} custom-call(s32[1]{0:T(128)} %bitcast.core, bf16[256,512]{1,0:T(8,128)(2,1)S(1)} %get-tuple-element.98.state, bf16[256,256]{1,0:T(8,128)(2,1)S(1)} %collective-permute-done.9.other, bf16[1024,256]{1,0:T(8,128)(2,1)S(1)} %get-tuple-element.105.in_mine, bf16[1024,256]{1,0:T(8,128)(2,1)S(1)} %get-tuple-element.106.in_other, ...), custom_call_target="tpu_custom_call" | custom-call | flops 402653184 | bytes 1048576 | tf_op jit(solution)/shard_map/node_last/pallas_call | solution.py:320
  (50 shorter events, 0.1 us)
Async XLA Ops:
  4.8 15.7 %copy-start.30 = (s32[1,2,64]{2,1,0:T(2,128)S(1)}, s32[1,2,64]{2,1,0:T(2,128)}, u32[]{:S(2)}) copy-start(s32[1,2,64]{2,1,0:T(2,128)} %param.25) | copy-start | bytes 1540
  4.9 15.7 %copy-start.26 = (s32[1,12288]{1,0:T(1,128)S(1)}, s32[1,12288]{1,0:T(1,128)}, u32[]{:S(2)}) copy-start(s32[1,12288]{1,0:T(1,128)} %param.24) | copy-start | bytes 147460
  4.9 40.6 %all-to-all-start = ((bf16[64,64,256]{2,1,0:T(8,128)(2,1)}), bf16[64,64,256]{2,1,0:T(8,128)(2,1)S(1)}, u32[]{:S(2)}, u32[]{:S(2)}) async-start(bf16[64,64,256]{2,1,0:T(8,128)(2,1)} %embed.1), calls=%async_computation | async-start | bytes 4194304 | tf_op jit(solution)/shard_map/all_to_all | solution.py:245
  17.0 12.4 %copy-start.23 = (bf16[2,512,256]{2,1,0:T(8,128)(2,1)S(1)}, bf16[2,512,256]{2,1,0:T(8,128)(2,1)}, u32[]{:S(2)}) copy-start(bf16[2,512,256]{2,1,0:T(8,128)(2,1)} %param.27) | copy-start | bytes 1572868
  17.0 12.3 %copy-start.24 = (bf16[2,512,256]{2,1,0:T(8,128)(2,1)S(1)}, bf16[2,512,256]{2,1,0:T(8,128)(2,1)}, u32[]{:S(2)}) copy-start(bf16[2,512,256]{2,1,0:T(8,128)(2,1)} %param.26) | copy-start | bytes 1572868
  17.0 19.4 %collective-permute-start.1 = (bf16[3,256]{1,0:T(4,128)(2,1)}, bf16[3,256]{1,0:T(4,128)(2,1)}, u32[]{:S(2)}, u32[]{:S(2)}) collective-permute-start(bf16[3,256]{1,0:T(4,128)(2,1)} %param.30), channel_id=1, source_target_pairs={{0,1},{1,0},{2,3},{3,2},{4,5},{5,4},{6,7},{7,6},{8,9},{9,8},{10,11... | collective-permute-start | bytes 4616 | tf_op jit(solution)/shard_map/ppermute | solution.py:201
  18.0 19.7 %collective-permute-start.2 = (bf16[3,256,512]{2,1,0:T(8,128)(2,1)}, bf16[3,256,512]{2,1,0:T(8,128)(2,1)}, u32[]{:S(2)}, u32[]{:S(2)}) collective-permute-start(bf16[3,256,512]{2,1,0:T(8,128)(2,1)} %param.31), channel_id=1, source_target_pairs={{0,1},{1,0},{2,3},{3,2},{4,5},{5,4},{6,7},{7,6},{8,9},{9,8},{10,11... | collective-permute-start | bytes 2359304 | tf_op jit(solution)/shard_map/ppermute | solution.py:201
  18.1 22.3 %collective-permute-start = (bf16[3,1024,256]{2,1,0:T(8,128)(2,1)}, bf16[3,1024,256]{2,1,0:T(8,128)(2,1)}, u32[]{:S(2)}, u32[]{:S(2)}) collective-permute-start(bf16[3,1024,256]{2,1,0:T(8,128)(2,1)} %param.29), channel_id=1, source_target_pairs={{0,1},{1,0},{2,3},{3,2},{4,5},{5,4},{6,7},{7,6},{8,9},{9,8},{10,11... | collective-permute-start | bytes 4718600 | tf_op jit(solution)/shard_map/ppermute | solution.py:201
  18.6 11.8 %copy-start.29 = (bf16[2,256]{1,0:T(2,128)(2,1)S(1)}, bf16[2,256]{1,0:T(2,128)(2,1)}, u32[]{:S(2)}) copy-start(bf16[2,256]{1,0:T(2,128)(2,1)} %param.28) | copy-start | bytes 3076
  28.7 3.1 %copy-start.22 = (bf16[3,1024,256]{2,1,0:T(8,128)(2,1)S(1)}, bf16[3,1024,256]{2,1,0:T(8,128)(2,1)}, u32[]{:S(2)}) copy-start(bf16[3,1024,256]{2,1,0:T(8,128)(2,1)} %param.29) | copy-start | bytes 4718596
  30.4 2.5 %copy-start.25 = (bf16[256,256]{1,0:T(8,128)(2,1)S(1)}, bf16[256,256]{1,0:T(8,128)(2,1)}, u32[]{:S(2)}) copy-start(bf16[256,256]{1,0:T(8,128)(2,1)} %param.17) | copy-start | bytes 393220
  30.4 4.5 %copy-start.27 = (s32[1,64,64]{2,1,0:T(8,128)S(1)}, s32[1,64,64]{2,1,0:T(8,128)}, u32[]{:S(2)}) copy-start(s32[1,64,64]{2,1,0:T(8,128)} %param.21) | copy-start | bytes 49156
  30.4 4.6 %copy-start.28 = (bf16[1,64,64]{2,1,0:T(8,128)(2,1)S(1)}, bf16[1,64,64]{2,1,0:T(8,128)(2,1)}, u32[]{:S(2)}) copy-start(bf16[1,64,64]{2,1,0:T(8,128)(2,1)} %param.22) | copy-start | bytes 24580
  45.4 3.3 %copy-start.2 = (bf16[1024,256]{1,0:T(8,128)(2,1)S(1)}, bf16[1024,256]{1,0:T(8,128)(2,1)}, u32[]{:S(2)}) copy-start(bf16[1024,256]{1,0:T(8,128)(2,1)} %get-tuple-element.68.in_mine) | copy-start | bytes 1572868
  45.4 3.3 %copy-start.3 = (bf16[1024,256]{1,0:T(8,128)(2,1)S(1)}, bf16[1024,256]{1,0:T(8,128)(2,1)}, u32[]{:S(2)}) copy-start(bf16[1024,256]{1,0:T(8,128)(2,1)} %get-tuple-element.69.in_other) | copy-start | bytes 1572868
  45.4 3.3 %copy-start.18 = (f32[1,256]{1,0:T(1,128)S(1)}, f32[1,256]{1,0:T(1,128)}, u32[]{:S(2)}) copy-start(f32[1,256]{1,0:T(1,128)} %get-tuple-element.70.bias_mine) | copy-start | bytes 3076
  45.4 3.3 %copy-start.21 = (f32[1,256]{1,0:T(1,128)S(1)}, f32[1,256]{1,0:T(1,128)}, u32[]{:S(2)}) copy-start(f32[1,256]{1,0:T(1,128)} %get-tuple-element.71.bias_other) | copy-start | bytes 3076
  45.4 4.3 %copy-start.5 = (bf16[256,512]{1,0:T(8,128)(2,1)S(1)}, bf16[256,512]{1,0:T(8,128)(2,1)}, u32[]{:S(2)}) copy-start(bf16[256,512]{1,0:T(8,128)(2,1)} %get-tuple-element.74.out_mine) | copy-start | bytes 786436
  45.5 4.3 %copy-start.7 = (bf16[256,512]{1,0:T(8,128)(2,1)S(1)}, bf16[256,512]{1,0:T(8,128)(2,1)}, u32[]{:S(2)}) copy-start(bf16[256,512]{1,0:T(8,128)(2,1)} %get-tuple-element.75.out_other) | copy-start | bytes 786436
  45.5 4.3 %copy-start.9 = (bf16[512,256]{1,0:T(8,128)(2,1)S(1)}, bf16[512,256]{1,0:T(8,128)(2,1)}, u32[]{:S(2)}) copy-start(bf16[512,256]{1,0:T(8,128)(2,1)} %get-tuple-element.76.send_w) | copy-start | bytes 786436
  45.5 4.3 %copy-start.15 = (f32[1,256]{1,0:T(1,128)S(1)}, f32[1,256]{1,0:T(1,128)}, u32[]{:S(2)}) copy-start(f32[1,256]{1,0:T(1,128)} %get-tuple-element.77.edge_bias) | copy-start | bytes 3076
  46.2 5.3 %copy-start.13 = (bf16[512,256]{1,0:T(8,128)(2,1)S(1)}, bf16[512,256]{1,0:T(8,128)(2,1)}, u32[]{:S(2)}) copy-start(bf16[512,256]{1,0:T(8,128)(2,1)} %get-tuple-element.83.recv_w) | copy-start | bytes 786436
  46.2 3.5 %collective-permute-start.3 = (bf16[256,256]{1,0:T(8,128)(2,1)S(1)}, bf16[256,256]{1,0:T(8,128)(2,1)S(1)}, u32[]{:S(2)}, u32[]{:S(2)}) collective-permute-start(bf16[256,256]{1,0:T(8,128)(2,1)S(1)} %slots.1.mine), channel_id=1, source_target_pairs={{0,1},{1,0},{2,3},{3,2},{4,5},{5,4},{6,7},{7,6},{8,9},{9,8},{10,11... | collective-permute-start | bytes 393224 | tf_op jit(solution)/shard_map/ppermute | solution.py:201
  50.5 5.5 %collective-permute-start.4 = (bf16[64,256]{1,0:T(8,128)(2,1)S(1)}, bf16[64,256]{1,0:T(8,128)(2,1)S(1)}, u32[]{:S(2)}, u32[]{:S(2)}) collective-permute-start(bf16[64,256]{1,0:T(8,128)(2,1)S(1)} %get-tuple-element.86), channel_id=1, source_target_pairs={{0,1},{1,0},{2,4},{3,5},{4,2},{5,3},{6,8},{7,9},{8,6},{9,7},{10,12... | collective-permute-start | bytes 98312 | tf_op jit(solution)/shard_map/ppermute | solution.py:329
  51.0 5.0 %collective-permute-start.5 = (bf16[64,256]{1,0:T(8,128)(2,1)S(1)}, bf16[64,256]{1,0:T(8,128)(2,1)S(1)}, u32[]{:S(2)}, u32[]{:S(2)}) collective-permute-start(bf16[64,256]{1,0:T(8,128)(2,1)S(1)} %get-tuple-element.87), channel_id=1, source_target_pairs={{0,2},{2,0},{4,6},{6,4},{8,10},{10,8},{12,14},{14,12},{16,18},{18,... | collective-permute-start | bytes 98312 | tf_op jit(solution)/shard_map/ppermute | solution.py:330
  56.0 2.8 %copy-start = (bf16[1024,256]{1,0:T(8,128)(2,1)S(1)}, bf16[1024,256]{1,0:T(8,128)(2,1)}, u32[]{:S(2)}) copy-start(bf16[1024,256]{1,0:T(8,128)(2,1)} %get-tuple-element.88.in_mine) | copy-start | bytes 1572868
  56.0 2.8 %copy-start.1 = (bf16[1024,256]{1,0:T(8,128)(2,1)S(1)}, bf16[1024,256]{1,0:T(8,128)(2,1)}, u32[]{:S(2)}) copy-start(bf16[1024,256]{1,0:T(8,128)(2,1)} %get-tuple-element.89.in_other) | copy-start | bytes 1572868
  56.1 2.8 %copy-start.17 = (f32[1,256]{1,0:T(1,128)S(1)}, f32[1,256]{1,0:T(1,128)}, u32[]{:S(2)}) copy-start(f32[1,256]{1,0:T(1,128)} %get-tuple-element.90.bias_mine) | copy-start | bytes 3076
  56.1 2.8 %copy-start.20 = (f32[1,256]{1,0:T(1,128)S(1)}, f32[1,256]{1,0:T(1,128)}, u32[]{:S(2)}) copy-start(f32[1,256]{1,0:T(1,128)} %get-tuple-element.91.bias_other) | copy-start | bytes 3076
  56.1 3.7 %copy-start.4 = (bf16[256,512]{1,0:T(8,128)(2,1)S(1)}, bf16[256,512]{1,0:T(8,128)(2,1)}, u32[]{:S(2)}) copy-start(bf16[256,512]{1,0:T(8,128)(2,1)} %get-tuple-element.94.out_mine) | copy-start | bytes 786436
  56.1 3.7 %copy-start.6 = (bf16[256,512]{1,0:T(8,128)(2,1)S(1)}, bf16[256,512]{1,0:T(8,128)(2,1)}, u32[]{:S(2)}) copy-start(bf16[256,512]{1,0:T(8,128)(2,1)} %get-tuple-element.95.out_other) | copy-start | bytes 786436
  56.1 3.7 %copy-start.8 = (bf16[512,256]{1,0:T(8,128)(2,1)S(1)}, bf16[512,256]{1,0:T(8,128)(2,1)}, u32[]{:S(2)}) copy-start(bf16[512,256]{1,0:T(8,128)(2,1)} %get-tuple-element.96.send_w) | copy-start | bytes 786436
  56.1 3.7 %copy-start.14 = (f32[1,256]{1,0:T(1,128)S(1)}, f32[1,256]{1,0:T(1,128)}, u32[]{:S(2)}) copy-start(f32[1,256]{1,0:T(1,128)} %get-tuple-element.97.edge_bias) | copy-start | bytes 3076
  57.8 5.6 %copy-start.12 = (bf16[512,256]{1,0:T(8,128)(2,1)S(1)}, bf16[512,256]{1,0:T(8,128)(2,1)}, u32[]{:S(2)}) copy-start(bf16[512,256]{1,0:T(8,128)(2,1)} %get-tuple-element.100.recv_w) | copy-start | bytes 786436
  57.8 2.0 %collective-permute-start.6 = (bf16[256,256]{1,0:T(8,128)(2,1)S(1)}, bf16[256,256]{1,0:T(8,128)(2,1)S(1)}, u32[]{:S(2)}, u32[]{:S(2)}) collective-permute-start(bf16[256,256]{1,0:T(8,128)(2,1)S(1)} %edge_halo.2.mine), channel_id=1, source_target_pairs={{0,1},{1,0},{2,3},{3,2},{4,5},{5,4},{6,7},{7,6},{8,9},{9,8},{10,11... | collective-permute-start | bytes 393224 | tf_op jit(solution)/shard_map/ppermute | solution.py:201
  60.6 7.2 %collective-permute-start.7 = (bf16[64,256]{1,0:T(8,128)(2,1)S(1)}, bf16[64,256]{1,0:T(8,128)(2,1)S(1)}, u32[]{:S(2)}, u32[]{:S(2)}) collective-permute-start(bf16[64,256]{1,0:T(8,128)(2,1)S(1)} %get-tuple-element.103), channel_id=1, source_target_pairs={{0,1},{1,0},{2,4},{3,5},{4,2},{5,3},{6,8},{7,9},{8,6},{9,7},{10,12... | collective-permute-start | bytes 98312 | tf_op jit(solution)/shard_map/ppermute | solution.py:329
  61.1 6.7 %collective-permute-start.8 = (bf16[64,256]{1,0:T(8,128)(2,1)S(1)}, bf16[64,256]{1,0:T(8,128)(2,1)S(1)}, u32[]{:S(2)}, u32[]{:S(2)}) collective-permute-start(bf16[64,256]{1,0:T(8,128)(2,1)S(1)} %get-tuple-element.104), channel_id=1, source_target_pairs={{0,2},{2,0},{4,6},{6,4},{8,10},{10,8},{12,14},{14,12},{16,18},{18,... | collective-permute-start | bytes 98312 | tf_op jit(solution)/shard_map/ppermute | solution.py:330
  67.8 2.8 %copy-start.16 = (f32[1,256]{1,0:T(1,128)S(1)}, f32[1,256]{1,0:T(1,128)}, u32[]{:S(2)}) copy-start(f32[1,256]{1,0:T(1,128)} %get-tuple-element.107.bias_mine) | copy-start | bytes 3076
  67.8 2.7 %copy-start.19 = (f32[1,256]{1,0:T(1,128)S(1)}, f32[1,256]{1,0:T(1,128)}, u32[]{:S(2)}) copy-start(f32[1,256]{1,0:T(1,128)} %get-tuple-element.108.bias_other) | copy-start | bytes 3076
  67.8 3.7 %copy-start.10 = (bf16[256,256]{1,0:T(8,128)(2,1)S(1)}, bf16[256,256]{1,0:T(8,128)(2,1)}, u32[]{:S(2)}) copy-start(bf16[256,256]{1,0:T(8,128)(2,1)} %dynamic-slice_bitcast_fusion.1.out_mine) | copy-start | bytes 393220
  67.9 3.7 %copy-start.11 = (bf16[256,256]{1,0:T(8,128)(2,1)S(1)}, bf16[256,256]{1,0:T(8,128)(2,1)}, u32[]{:S(2)}) copy-start(bf16[256,256]{1,0:T(8,128)(2,1)} %dynamic-slice_bitcast_fusion.out_other) | copy-start | bytes 393220
  69.6 2.0 %collective-permute-start.9 = (bf16[256,256]{1,0:T(8,128)(2,1)S(1)}, bf16[256,256]{1,0:T(8,128)(2,1)S(1)}, u32[]{:S(2)}, u32[]{:S(2)}) collective-permute-start(bf16[256,256]{1,0:T(8,128)(2,1)S(1)} %edge_halo.3.mine), channel_id=1, source_target_pairs={{0,1},{1,0},{2,3},{3,2},{4,5},{5,4},{6,7},{7,6},{8,9},{9,8},{10,11... | collective-permute-start | bytes 393224 | tf_op jit(solution)/shard_map/ppermute | solution.py:201
